TPU v7x, 32 devices: a whole 2x2x4 slice. The times are simulated.
32 devices in a mesh: book: 2 (over y), trade: 8 (over z, x), path: 2 (over core).
Axes of the slice: x: 2, y: 2, z: 4, core: 2. Of those that a mesh axis runs over, the one named last changes fastest.
Arguments:
- shocks: float32 [4, 2, 2, 8], P('book', None, 'path', 'trade'), parts along dimension 0, may hold values from -6 to 6
- trade_kind: int32 [8192, 16], P(('book', 'trade')), parts along dimension 0, may hold values from 0 to 2
- cash_start: int32 [8192, 16], P(('book', 'trade')), parts along dimension 0, may hold values from 3 to 34
- cash_count: int32 [8192, 16], P(('book', 'trade')), parts along dimension 0, may hold values from 4 to 63
- strike: float32 [8192, 16], P(('book', 'trade')), parts along dimension 0, may hold values from 0.005 to 0.05
- normal_vol: float32 [8192, 16], P(('book', 'trade')), parts along dimension 0, may hold values from 0.004 to 0.015
- notional: float32 [8192, 16], P(('book', 'trade')), parts along dimension 0, may hold values from -4 to 4
- block_count: int32 [8192], P(('book', 'trade')), parts along dimension 0, may hold values from 1 to 16
- block_set: int32 [8192], P(('book', 'trade')), parts along dimension 0, may hold values from 0 to 255, as said below
Outputs:
- exposure: float32 [512, 2, 16], P(('book', 'trade'), None, 'path'), parts along dimension 0
There are 2 independent parts, one for each index of `book`. A program takes and returns all parts, laid end to end along the dimension named above; each array names one. Nothing has to cross between parts.
Inputs may be any that keep to these rules, and one draw needn't show every extreme that they name: `block_set`: trade block b has its netting set s with s // 32 == (b % 512) // 64: the blocks of one device are ordered by the device that owns their set, 64 blocks to each.
All inputs are finite; a program needn't handle non-finite values.
Results may differ from a plain program's by a relative error of at most 0.0003.
Values sent between devices are 32-bit elements; how exact they have to be, the bound alone decides.
No kernel may reach another device: no remote copies, remote signals or barrier semaphores. Data moves between devices by JAX's collectives and lax.ppermute only.
A program may use at most 64 MiB of HBM per device.

v0:
```python
import math

import jax
import jax.numpy as jnp
from jax import lax
from jax.sharding import PartitionSpec as P

GRID = 128
SET_DEV = 32


YEAR_STEP = 0.25
FLAT_RATE = 0.03
REVERT_FAST = 0.5
REVERT_SLOW = 0.04
VOL_FAST = 0.012
VOL_SLOW = 0.009
FACTOR_CORR = -0.6
HIGHEST = lax.Precision.HIGHEST


def loading(reversion, horizon):
    return (1.0 - jnp.exp(-reversion * horizon)) / reversion


def one_variance(reversion, volatility, horizon):
    return (
        volatility**2
        / reversion**2
        * (
            horizon
            + 2.0 / reversion * jnp.exp(-reversion * horizon)
            - 0.5 / reversion * jnp.exp(-2.0 * reversion * horizon)
            - 1.5 / reversion
        )
    )


def factor_variance(horizon):
    fast_part = one_variance(REVERT_FAST, VOL_FAST, horizon)
    slow_part = one_variance(REVERT_SLOW, VOL_SLOW, horizon)
    both_rates = REVERT_FAST + REVERT_SLOW
    cross_part = (
        2.0
        * FACTOR_CORR
        * VOL_FAST
        * VOL_SLOW
        / (REVERT_FAST * REVERT_SLOW)
        * (
            horizon
            + (jnp.exp(-REVERT_FAST * horizon) - 1.0) / REVERT_FAST
            + (jnp.exp(-REVERT_SLOW * horizon) - 1.0) / REVERT_SLOW
            - (jnp.exp(-both_rates * horizon) - 1.0) / both_rates
        )
    )
    return fast_part + slow_part + cross_part


def evolve(path_shocks):
    fast_keep = math.exp(-REVERT_FAST * YEAR_STEP)
    slow_keep = math.exp(-REVERT_SLOW * YEAR_STEP)
    fast_scale = VOL_FAST * math.sqrt(
        (1.0 - math.exp(-2.0 * REVERT_FAST * YEAR_STEP)) / (2.0 * REVERT_FAST)
    )
    slow_scale = VOL_SLOW * math.sqrt(
        (1.0 - math.exp(-2.0 * REVERT_SLOW * YEAR_STEP)) / (2.0 * REVERT_SLOW)
    )
    mixing = math.sqrt(1.0 - FACTOR_CORR**2)
    fast_state = jnp.zeros(path_shocks.shape[2:], jnp.float32)
    slow_state = jnp.zeros(path_shocks.shape[2:], jnp.float32)
    fast_path = []
    slow_path = []
    for period in range(path_shocks.shape[1]):
        fast_state = fast_state * fast_keep + fast_scale * path_shocks[0, period]
        slow_state = slow_state * slow_keep + slow_scale * (
            FACTOR_CORR * path_shocks[0, period] + mixing * path_shocks[1, period]
        )
        fast_path.append(fast_state)
        slow_path.append(slow_state)
    return jnp.stack([jnp.stack(fast_path), jnp.stack(slow_path)])


def discount_table(states):
    dates_count = states.shape[1]
    maturity = lax.broadcasted_iota(jnp.int32, (GRID, 1, 1), 0).astype(jnp.float32) * YEAR_STEP
    valued = (lax.broadcasted_iota(jnp.int32, (1, dates_count, 1), 1) + 1).astype(
        jnp.float32
    ) * YEAR_STEP
    horizon = maturity - valued
    log_front = -FLAT_RATE * horizon + 0.5 * (
        factor_variance(horizon) - factor_variance(maturity) + factor_variance(valued)
    )
    return jnp.exp(
        log_front
        - loading(REVERT_FAST, horizon) * states[0][None]
        - loading(REVERT_SLOW, horizon) * states[1][None]
    )


def price_blocks(
    trade_kind,
    cash_start,
    cash_count,
    strike,
    normal_vol,
    notional,
    block_count,
    discounts,
    dates_count,
):
    groups, slot_count = cash_start.shape
    cash_nodes = lax.broadcasted_iota(jnp.int32, (1, 1, GRID), 2)
    first_node = cash_start[:, :, None]
    last_node = (cash_start + cash_count)[:, :, None]
    accrual = jnp.where(
        (cash_nodes > first_node) & (cash_nodes <= last_node), YEAR_STEP, 0.0
    ).astype(jnp.float32)
    endpoints = (
        jnp.where(cash_nodes == first_node, 1.0, 0.0) - jnp.where(cash_nodes == last_node, 1.0, 0.0)
    ).astype(jnp.float32)
    weights = jnp.concatenate([accrual, endpoints], axis=0).reshape(2 * groups * slot_count, GRID)
    products = jnp.dot(weights, discounts, precision=HIGHEST, preferred_element_type=jnp.float32)
    products = products.reshape(2, groups, slot_count, dates_count, -1)
    annuity = products[0]
    float_leg = products[1]
    swap_rate = float_leg / annuity
    valued = (lax.broadcasted_iota(jnp.int32, (1, 1, dates_count, 1), 2) + 1).astype(
        jnp.float32
    ) * YEAR_STEP
    expiry = cash_start.astype(jnp.float32)[:, :, None, None] * YEAR_STEP
    spread = normal_vol[:, :, None, None] * jnp.sqrt(expiry - valued)
    moneyness = swap_rate - strike[:, :, None, None]
    standard = moneyness / spread
    normal_cdf = 0.5 * (1.0 + jax.scipy.special.erf(standard * (1.0 / math.sqrt(2.0))))
    normal_pdf = jnp.exp(-0.5 * standard * standard) * (1.0 / math.sqrt(2.0 * math.pi))
    offset = jnp.where(trade_kind == 1, 1.0, jnp.where(trade_kind == 2, 0.5, 0.0))[:, :, None, None]
    factor = (jnp.where(trade_kind == 2, 2.0, 1.0) * notional)[:, :, None, None]
    trade_value = factor * annuity * (moneyness * (normal_cdf - offset) + spread * normal_pdf)
    occupied = lax.broadcasted_iota(jnp.int32, (groups, slot_count), 1) < block_count[:, None]
    trade_value = jnp.where(occupied[:, :, None, None], trade_value, 0.0)
    return jnp.sum(trade_value, axis=1).reshape(groups, -1)


def price_all(fields, discounts, dates_count):
    block_rows = fields[0].shape[0]
    group_size = max(32, block_rows // 16)
    turns = block_rows // group_size

    def regroup(array):
        return array.reshape((turns, group_size) + array.shape[1:])

    def one_group(pieces):
        return price_blocks(
            pieces[0],
            pieces[1],
            pieces[2],
            pieces[3],
            pieces[4],
            pieces[5],
            pieces[6],
            discounts,
            dates_count,
        )

    totals = lax.map(one_group, tuple((regroup(field) for field in fields)))
    return totals.reshape(block_rows, -1)


def shards(
    shocks, trade_kind, cash_start, cash_count, strike, normal_vol, notional, block_count, block_set
):
    dates_count = shocks.shape[1]
    own_states = evolve(shocks.reshape(2, dates_count, -1))
    gathered = lax.all_gather(own_states, "trade", axis=2, tiled=True)
    discounts = discount_table(gathered)
    discounts = discounts.reshape(GRID, -1)
    block_total = price_all(
        (trade_kind, cash_start, cash_count, strike, normal_vol, notional, block_count),
        discounts,
        dates_count,
    )
    set_index = lax.broadcasted_iota(jnp.int32, (SET_DEV * lax.axis_size("trade"), 1), 0)
    one_hot = (set_index == block_set[None, :]).astype(jnp.float32)
    netted = lax.psum_scatter(
        jnp.dot(one_hot, block_total, precision=HIGHEST, preferred_element_type=jnp.float32),
        "trade",
        scatter_dimension=0,
        tiled=True,
    )
    return jnp.maximum(netted, 0.0).reshape(SET_DEV, dates_count, -1)


def solution(mesh):
    placed = (
        P("book", None, "path", "trade"),
        P(("book", "trade"), None),
        P(("book", "trade"), None),
        P(("book", "trade"), None),
        P(("book", "trade"), None),
        P(("book", "trade"), None),
        P(("book", "trade"), None),
        P(("book", "trade")),
        P(("book", "trade")),
    )
    return jax.shard_map(
        shards,
        mesh=mesh,
        in_specs=placed,
        out_specs=P(("book", "trade"), None, "path"),
        check_vma=False,
    )
```

profile of v0, /device:TPU:0, one launch (start us, length us, event | category | flops | bytes accessed | tf_op | source)
XLA Modules:
  0.0 135.6 jit_solution(14833694432791545668)
XLA Ops:
  6.5 0.7 copy-done.6
  7.2 0.6 fusion.47
  12.4 22.2 %all_gather.3 = f32[2,2,8]{1,0,2:T(2,128)S(1)} all-gather(f32[2,2,1]{1,0,2:T(2,128)S(1)} %bitcast.100), channel_id=1, replica_groups=mesh['book'=2,'trade'=8,'path'=2] {'trade'}, dimensions={2}, use_global_device_ids=true | all-gather | bytes 144 | tf_op jit(solution)/shard_map/all_gather | solution.py:174
  35.1 0.6 copy-done.1
  35.8 0.6 copy-done.2
  36.6 0.6 copy-done.3
  37.4 0.6 copy-done.4
  38.1 0.6 copy-done.5
  38.9 0.6 copy-done.7
  39.6 27.8 %while.11 = (s32[]{:T(128)}, f32[16,32,16]{1,0,2:T(8,128)S(1)}, s32[16,32]{1,0:T(8,128)S(1)}, s32[16,32,16]{2,1,0:T(8,128)S(1)}, f32[16,32,16]{2,1,0:T(8,128)S(1...) while((s32[]{:T(128)}, f32[16,32,16]{1,0,2:T(8,128)S(1)}, ...), condition=%wide.region_2.3_spmd.clone, body=%wide.region_0.2_spmd.clone.sunk | while | flops 26033672 | bytes 2563777 | solution.py:165
  39.9 0.5 fusion.60
  41.6 0.5 fusion.60
  43.4 0.5 fusion.60
  45.1 0.5 fusion.60
  46.9 0.5 fusion.60
  48.6 0.5 fusion.60
  50.3 0.5 fusion.60
  62.5 0.6 fusion.60
  64.2 0.6 fusion.60
  67.5 0.6 copy-done.8
  68.1 1.0 fusion.23
  69.1 58.3 %reduce-scatter.4.cloned.1.call-done = f32[32,16]{1,0:T(8,128)} async-done(((f32[256,16]{1,0:T(8,128)}), f32[32,16]{1,0:T(8,128)}) %reduce-scatter.4.cloned.1.call-update) | async-done | bytes 2064
  127.4 0.8 copy.62
  128.2 0.6 maximum_bitcast_fusion
  (295 shorter events, 22.5 us)
Async XLA Ops:
  6.5 0.7 copy-start.6
  6.5 120.9 %reduce-scatter.4.cloned.1.call-start = ((), (), s32[]{:S(2)}) async-start(), calls=%async_computation.1 | async-start | bytes 147456
  12.1 22.8 %copy-start = (s32[512,16]{0,1:T(8,128)S(1)}, s32[512,16]{0,1:T(8,128)}, u32[]{:S(2)}) copy-start(s32[512,16]{0,1:T(8,128)} %param.12) | copy-start | bytes 98308
  35.0 0.8 copy-start.1
  35.7 0.8 copy-start.2
  36.5 0.8 copy-start.3
  37.2 0.8 copy-start.4
  38.0 0.8 copy-start.5
  38.8 0.7 copy-start.7
  67.4 0.7 copy-start.8
Sparse Core Ops, SparseCore 0:
  69.2 58.1 reduce-scatter.3
where the time goes:
time: 136 us
  waiting for transfers between devices  58.3 us (43%)
  blocking collectives  22.2 us (16%)
  between operations  17.7 us (13%)
  local copies, waits for them, and re-layouts  13.1 us (10%)
  other arithmetic  12.5 us (9%)
  matrix products  9.83 us (7%)
  loops' own time  1.92 us (1%)
    unnamed x2, waiting for transfers between devices  58.3 us
    all_gather x1, blocking collectives, shards(): gathered = lax.all_gather(own_states, 'trade', axis=2, tiled=True)  22.2 us
    dot_general x16, matrix products, price_blocks(): jnp.dot(weights, discounts, precision=HIGHEST, preferred_element_type=jnp...  8.83 us
    unnamed x25, local copies, waits for them, and re-layouts  6.46 us
    reduce_sum x16, other arithmetic, price_blocks(): return jnp.sum(trade_value, axis=1).reshape(groups, -1)  4.3 us
    select_n x16, other arithmetic, price_blocks(): jnp.where((cash_nodes > first_node) & (cash_nodes <= last_node), YEAR_STE...  3.23 us
  transfers between devices with their start and end apart: 1, of which 1 were waited for; matrix products, arithmetic and copies ran while one was open for 0% of the time, Pallas kernels for 0%

commit v1 on v0

--- a/solution.py
+++ b/solution.py
@@ -3,6 +3,8 @@
 import jax
 import jax.numpy as jnp
 from jax import lax
+from jax.experimental import pallas as pl
+from jax.experimental.pallas import tpu as pltpu
 from jax.sharding import PartitionSpec as P
 
 GRID = 128
@@ -166,7 +168,7 @@
     return totals.reshape(block_rows, -1)
 
 
-def shards(
+def shards_by_sum(
     shocks, trade_kind, cash_start, cash_count, strike, normal_vol, notional, block_count, block_set
 ):
     dates_count = shocks.shape[1]
@@ -190,6 +192,213 @@
     return jnp.maximum(netted, 0.0).reshape(SET_DEV, dates_count, -1)
 
 
+SLOTS_TILE = 8
+LANES = 128
+FIELDS = 6
+ROWS = (FIELDS + 1) * SLOTS_TILE
+DATES = 2
+
+TAIL = (
+    -1.325748085975647,
+    -1.8081499338150024,
+    -0.4117443561553955,
+    -0.0426594540476799,
+    0.0026849275454878807,
+    0.0004979888908565044,
+    -0.00017640502483118325,
+    2.543121991038788e-05,
+    -1.9144790712743998e-06,
+    6.075951120010359e-08,
+)
+TAIL_END = 10.0
+
+
+def iota(shape, dimension):
+    return lax.broadcasted_iota(jnp.int32, shape, dimension)
+
+
+def pack(kind, start, count, strike, vol, notional, live, group, shocks, out):
+    slot_count, blocks = start.shape
+    half = LANES // 2
+    low = iota((SLOTS_TILE, LANES), 1) < half
+    row = iota((SLOTS_TILE, LANES), 0)
+    first = start[...]
+    kinds = kind[...]
+    occupied = iota((slot_count, blocks), 0) < live[...]
+    fields = (
+        first.astype(jnp.float32),
+        (first + count[...]).astype(jnp.float32),
+        strike[...],
+        vol[...],
+        jnp.where(occupied, jnp.where(kinds == 2, 2.0, 1.0) * notional[...], 0.0),
+        jnp.where(kinds == 1, 1.0, jnp.where(kinds == 2, 0.5, 0.0)),
+    )
+    sets = jnp.broadcast_to((group[...] % SET_DEV).astype(jnp.float32), (SLOTS_TILE, blocks))
+    extra = jnp.zeros((SLOTS_TILE, LANES), jnp.float32)
+    for factor in range(2):
+        for date in range(DATES):
+            value = jnp.broadcast_to(shocks[factor : factor + 1, date : date + 1], (SLOTS_TILE, LANES))
+            extra = jnp.where(row == 1 + factor * DATES + date, value, extra)
+    for pair in range(blocks // LANES):
+        cut = slice(pair * LANES, (pair + 1) * LANES)
+        for at, field in enumerate(fields):
+            top, bottom = field[:SLOTS_TILE, cut], field[SLOTS_TILE:, cut]
+            here = slice(at * SLOTS_TILE, (at + 1) * SLOTS_TILE)
+            out[2 * pair, here, :] = jnp.where(low, top, pltpu.roll(bottom, half, 1))
+            out[2 * pair + 1, here, :] = jnp.where(low, pltpu.roll(top, half, 1), bottom)
+        own = sets[:, cut]
+        turned = pltpu.roll(own, half, 1)
+        here = slice(FIELDS * SLOTS_TILE, ROWS)
+        out[2 * pair, here, :] = jnp.where(row == 0, jnp.where(low, own, turned), extra)
+        out[2 * pair + 1, here, :] = jnp.where(row == 0, jnp.where(low, turned, own), extra)
+
+
+def split(values):
+    parts = []
+    for _ in range(3):
+        part = values.astype(jnp.bfloat16)
+        parts.append(part)
+        values = values - part.astype(jnp.float32)
+    return parts
+
+
+def tables(shocks):
+    node = iota((1, GRID), 1).astype(jnp.float32) * YEAR_STEP
+    states = evolve(shocks)
+    discounts = []
+    for date in range(DATES):
+        valued = (date + 1) * YEAR_STEP
+        horizon = node - valued
+        front = -FLAT_RATE * horizon + 0.5 * (
+            factor_variance(horizon) - factor_variance(node) + factor_variance(jnp.full((1, GRID), valued))
+        )
+        discounts.append(
+            jnp.exp(
+                front
+                - loading(REVERT_FAST, horizon) * states[0, date]
+                - loading(REVERT_SLOW, horizon) * states[1, date]
+            )
+        )
+    both = jnp.concatenate(discounts, axis=0)
+    mid = GRID // 4
+    source, target = iota((GRID, GRID), 0), iota((GRID, GRID), 1)
+    weights = jnp.where((source > mid) & (source <= target), YEAR_STEP, 0.0) - jnp.where(
+        (source <= mid) & (source > target), YEAR_STEP, 0.0
+    )
+    weights = weights.astype(jnp.bfloat16)
+    sums = sum(
+        jnp.dot(part, weights, preferred_element_type=jnp.float32) for part in reversed(split(both))
+    )
+    return both, sums
+
+
+def price(ref, out, discount, running, totals):
+    sources = ref.shape[0]
+    extra = FIELDS * SLOTS_TILE
+    shocks = jnp.stack(
+        [jnp.stack([ref[:, extra + 1 + factor * DATES + date, :] for date in range(DATES)]) for factor in range(2)]
+    )
+    discount[...], running[...] = tables(shocks)
+    row = iota((SLOTS_TILE, LANES), 0)
+    masks = [(row & bit) == 0 for bit in (1, 2, 4)]
+
+    def one_source(source, carry):
+        def field(at):
+            return ref[source, at * SLOTS_TILE : (at + 1) * SLOTS_TILE, :]
+
+        first, last = field(0), field(1)
+        first_node, last_node = first.astype(jnp.int32), last.astype(jnp.int32)
+        strike, vol, size, offset = field(2), field(3), field(4), field(5)
+        tilt = 0.5 - offset
+        for date in range(DATES):
+            spread = vol * jnp.sqrt(first * YEAR_STEP - (date + 1) * YEAR_STEP)
+            inverse = 1.0 / spread
+            scale = size * spread
+            values = []
+            for path in range(SLOTS_TILE):
+                at = date * SLOTS_TILE + path
+                curve = jnp.broadcast_to(discount[at : at + 1, :], (SLOTS_TILE, LANES))
+                sums = jnp.broadcast_to(running[at : at + 1, :], (SLOTS_TILE, LANES))
+                float_leg = jnp.take_along_axis(curve, first_node, axis=1) - jnp.take_along_axis(
+                    curve, last_node, axis=1
+                )
+                annuity = jnp.take_along_axis(sums, last_node, axis=1) - jnp.take_along_axis(
+                    sums, first_node, axis=1
+                )
+                standard = (float_leg / annuity - strike) * inverse
+                size_of = jnp.abs(standard)
+                capped = jnp.minimum(size_of, TAIL_END)
+                power = jnp.full_like(capped, TAIL[-1])
+                for term in TAIL[-2::-1]:
+                    power = power * capped + term
+                tail = jnp.exp2(power)
+                values.append(scale * annuity * (0.5 * size_of + tilt * standard + tail))
+            for bit, mask in zip((1, 2, 4), masks):
+                values = [
+                    jnp.where(mask, a, b) + pltpu.roll(jnp.where(mask, b, a), bit, 0)
+                    for a, b in zip(values[::2], values[1::2])
+                ]
+            totals[source, date * SLOTS_TILE : (date + 1) * SLOTS_TILE, :] = values[0]
+        return carry
+
+    lax.fori_loop(0, sources, one_source, 0)
+    set_index = iota((SET_DEV, LANES), 0).astype(jnp.float32)
+    netted = jnp.zeros((DATES * SLOTS_TILE, SET_DEV), jnp.float32)
+    for source in range(sources):
+        one_hot = (set_index == ref[source, extra : extra + 1, :]).astype(jnp.float32)
+        netted = netted + lax.dot_general(
+            totals[source],
+            one_hot,
+            (((1,), (1,)), ((), ())),
+            precision=HIGHEST,
+            preferred_element_type=jnp.float32,
+        )
+    out[...] = jnp.maximum(netted, 0.0)
+
+
+def shards_by_trade(
+    shocks, trade_kind, cash_start, cash_count, strike, normal_vol, notional, block_count, block_set
+):
+    dates_count = shocks.shape[1]
+    owners = lax.axis_size("trade")
+    message = pl.pallas_call(
+        pack, out_shape=jax.ShapeDtypeStruct((owners, ROWS, LANES), jnp.float32), name="pack"
+    )(
+        trade_kind.T,
+        cash_start.T,
+        cash_count.T,
+        strike.T,
+        normal_vol.T,
+        notional.T,
+        block_count.reshape(1, -1),
+        block_set.reshape(1, -1),
+        shocks.reshape(2, dates_count),
+    )
+    received = lax.all_to_all(message, "trade", 0, 0, tiled=True)
+    netted = pl.pallas_call(
+        price,
+        out_shape=jax.ShapeDtypeStruct((dates_count * SLOTS_TILE, SET_DEV), jnp.float32),
+        scratch_shapes=[
+            pltpu.VMEM((dates_count * SLOTS_TILE, GRID), jnp.float32),
+            pltpu.VMEM((dates_count * SLOTS_TILE, GRID), jnp.float32),
+            pltpu.VMEM((owners, dates_count * SLOTS_TILE, LANES), jnp.float32),
+        ],
+        name="price",
+    )(received)
+    return netted.reshape(dates_count, SLOTS_TILE, SET_DEV).transpose(2, 0, 1)
+
+
+def shards(shocks, trade_kind, *others):
+    blocks, slot_count = trade_kind.shape
+    by_trade = (
+        lax.axis_size("trade") == SLOTS_TILE
+        and shocks.shape == (2, DATES, 1, 1)
+        and slot_count == 2 * SLOTS_TILE
+        and blocks == SLOTS_TILE * LANES // 2
+    )
+    return (shards_by_trade if by_trade else shards_by_sum)(shocks, trade_kind, *others)
+
+
 def solution(mesh):
     placed = (
         P("book", None, "path", "trade"),

time: 136 us -> 21.8 us (0.16)
  waiting for transfers between devices: 58.3 us -> 0 us
  between operations: 17.7 us -> 0.01 us
  local copies, waits for them, and re-layouts: 13.1 us -> 0 us
  other arithmetic: 12.5 us -> 0 us
  matrix products: 9.83 us -> 0 us
  blocking collectives: 22.2 us -> 15.8 us
  Pallas kernels: 0 us -> 5.72 us
  loops' own time: 1.92 us -> 0 us
    unnamed x2 -> x0, waiting for transfers between devices: 58.3 us -> none
    all_gather x1 -> x0, blocking collectives: 22.2 us -> none  [shards(): gathered = lax.all_gather(own_states, 'trade', axis=2, tiled=True)]
    all_to_all x0 -> x1, blocking collectives: none -> 15.8 us  [shards_by_trade(): received = lax.all_to_all(message, 'trade', 0, 0, tiled=True)]
    dot_general x16 -> x0, matrix products: 8.83 us -> none  [price_blocks(): jnp.dot(weights, discounts, precision=HIGHEST, preferred_element_type=jnp...]
    unnamed x25 -> x0, local copies, waits for them, and re-layouts: 6.46 us -> none
    pallas_call x0 -> x2, Pallas kernels: none -> 5.72 us  [the longest x1 4.06 us: shards_by_trade(): pl.pallas_call(price, out_shape=jax.ShapeDtypeStruct((dates_count * SLOTS...]
    reduce_sum x16 -> x0, other arithmetic: 4.3 us -> none  [price_blocks(): return jnp.sum(trade_value, axis=1).reshape(groups, -1)]
    squeeze x32 -> x0, local copies, waits for them, and re-layouts: 3.88 us -> none  [the longest x16 1.95 us: price_blocks(): float_leg = products[1]]
  transfers between devices with their start and end apart: 1 -> 0, of which waited for: 1 -> 0; matrix products, arithmetic and copies ran while one was open for 0% -> 0% of each run, Pallas kernels for 0% -> 0%
where the time goes in v1:
time: 21.8 us; the launch traced here: 21.5 us
  blocking collectives  15.8 us (72%)
  Pallas kernels  5.72 us (26%)
    all_to_all x1, blocking collectives, shards_by_trade(): received = lax.all_to_all(message, 'trade', 0, 0, tiled=True)  15.8 us
    pallas_call x1, Pallas kernels, shards_by_trade(): pl.pallas_call(price, out_shape=jax.ShapeDtypeStruct((dates_count * SLOTS...  4.06 us
    pallas_call x1, Pallas kernels, shards_by_trade(): pl.pallas_call(pack, out_shape=jax.ShapeDtypeStruct((owners, ROWS, LANES)...  1.66 us

profile of v1, /device:TPU:0, one launch (start us, length us, event | category | flops | bytes accessed | tf_op | source)
XLA Modules:
  0.0 21.5 jit_solution(15172639867577780268)
XLA Ops:
  0.0 1.7 %pack.1 = f32[8,56,128]{2,1,0:T(8,128)} custom-call(s32[16,512]{1,0:T(8,128)} %bitcast.12, s32[16,512]{1,0:T(8,128)} %bitcast.13, s32[16,512]{1,0:T(8,128)} %bitcast.14, f32[16,512]{1,0:T(8,128)} %bitcast.15, f32[16,512]{1,0:T(8,128)} %bitcast.16, f32[16,512]{1,0:T(8,128)} %bitcast.17, s32[1,512]{1,0:T(1,128)} %bitcast.18, s32[1,512]{1,0:T(1,128)} %bitcast.19, ...), custom_call_target="tpu_custom_call" | custom-call | tf_op jit(solution)/shard_map/pack/pallas_call | solution.py:364
  1.7 15.8 %all_to_all.5.ref = f32[8,56,128]{2,1,0:T(8,128)} all-to-all(f32[8,56,128]{2,1,0:T(8,128)} %pack.1), channel_id=1, replica_groups=mesh['book'=2,'trade'=8,'path'=2] {'trade'}, dimensions={0} | all-to-all | bytes 458752 | tf_op jit(solution)/shard_map/all_to_all | solution.py:377
  17.5 4.1 %price.1 = f32[16,32]{1,0:T(8,128)} custom-call(f32[8,56,128]{2,1,0:T(8,128)} %all_to_all.5.ref), custom_call_target="tpu_custom_call" | custom-call | tf_op jit(solution)/shard_map/price/pallas_call | solution.py:378

commit v2 on v1

--- a/solution.py
+++ b/solution.py
@@ -197,6 +197,7 @@
 FIELDS = 6
 ROWS = (FIELDS + 1) * SLOTS_TILE
 DATES = 2
+VMEM_BYTES = 8 * 2**20
 
 TAIL = (
     -1.325748085975647,
@@ -217,7 +218,18 @@
     return lax.broadcasted_iota(jnp.int32, shape, dimension)
 
 
-def pack(kind, start, count, strike, vol, notional, live, group, shocks, out):
+def pack(*refs):
+    count_of = len(refs) // 2 - 1
+    sources, out, held, arrived = refs[:count_of], refs[count_of], refs[count_of + 1 : -1], refs[-1]
+    copies = [
+        pltpu.make_async_copy(source, target, arrived.at[at])
+        for at, (source, target) in enumerate(zip(sources, held))
+    ]
+    for copy in copies:
+        copy.start()
+    for copy in copies:
+        copy.wait()
+    kind, start, count, strike, vol, notional, live, group, shocks = held
     slot_count, blocks = start.shape
     half = LANES // 2
     low = iota((SLOTS_TILE, LANES), 1) < half
@@ -341,7 +353,8 @@
             totals[source, date * SLOTS_TILE : (date + 1) * SLOTS_TILE, :] = values[0]
         return carry
 
-    lax.fori_loop(0, sources, one_source, 0)
+    for source in range(sources):
+        one_source(source, 0)
     set_index = iota((SET_DEV, LANES), 0).astype(jnp.float32)
     netted = jnp.zeros((DATES * SLOTS_TILE, SET_DEV), jnp.float32)
     for source in range(sources):
@@ -361,9 +374,7 @@
 ):
     dates_count = shocks.shape[1]
     owners = lax.axis_size("trade")
-    message = pl.pallas_call(
-        pack, out_shape=jax.ShapeDtypeStruct((owners, ROWS, LANES), jnp.float32), name="pack"
-    )(
+    fields = (
         trade_kind.T,
         cash_start.T,
         cash_count.T,
@@ -374,6 +385,15 @@
         block_set.reshape(1, -1),
         shocks.reshape(2, dates_count),
     )
+    message = pl.pallas_call(
+        pack,
+        out_shape=jax.ShapeDtypeStruct((owners, ROWS, LANES), jnp.float32),
+        in_specs=[pl.BlockSpec(memory_space=pltpu.HBM)] * len(fields),
+        scratch_shapes=[pltpu.VMEM(field.shape, field.dtype) for field in fields]
+        + [pltpu.SemaphoreType.DMA((len(fields),))],
+        compiler_params=pltpu.CompilerParams(vmem_limit_bytes=VMEM_BYTES),
+        name="pack",
+    )(*(pltpu.with_memory_space_constraint(field, pltpu.HBM) for field in fields))
     received = lax.all_to_all(message, "trade", 0, 0, tiled=True)
     netted = pl.pallas_call(
         price,
@@ -384,6 +404,7 @@
             pltpu.VMEM((owners, dates_count * SLOTS_TILE, LANES), jnp.float32),
         ],
         name="price",
+        compiler_params=pltpu.CompilerParams(vmem_limit_bytes=VMEM_BYTES),
     )(received)
     return netted.reshape(dates_count, SLOTS_TILE, SET_DEV).transpose(2, 0, 1)
 

time: 21.8 us -> 18.8 us (0.86)
  Pallas kernels: 5.72 us -> 3.1 us
  blocking collectives: 15.8 us -> 15.5 us
    pallas_call x1, Pallas kernels: 4.06 us -> 2.06 us  [shards_by_trade(): pl.pallas_call(price, out_shape=jax.ShapeDtypeStruct((dates_count * SLOTS...]
    pallas_call x1, Pallas kernels: 1.66 us -> 1.05 us  [shards_by_trade(): pl.pallas_call(pack, out_shape=jax.ShapeDtypeStruct((owners, ROWS, LANES)...]
    all_to_all x1, blocking collectives: 15.8 us -> 15.5 us  [shards_by_trade(): received = lax.all_to_all(message, 'trade', 0, 0, tiled=True)]
where the time goes in v2:
time: 18.8 us; the launch traced here: 18.6 us
  blocking collectives  15.5 us (82%)
  Pallas kernels  3.1 us (16%)
    all_to_all x1, blocking collectives, shards_by_trade(): received = lax.all_to_all(message, 'trade', 0, 0, tiled=True)  15.5 us
    pallas_call x1, Pallas kernels, shards_by_trade(): pl.pallas_call(price, out_shape=jax.ShapeDtypeStruct((dates_count * SLOTS...  2.06 us
    pallas_call x1, Pallas kernels, shards_by_trade(): pl.pallas_call(pack, out_shape=jax.ShapeDtypeStruct((owners, ROWS, LANES)...  1.05 us

profile of v2, /device:TPU:0, one launch (start us, length us, event | category | flops | bytes accessed | tf_op | source)
XLA Modules:
  0.0 18.6 jit_solution(7546775827810764746)
XLA Ops:
  0.0 1.0 %pack.1 = f32[8,56,128]{2,1,0:T(8,128)S(1)} custom-call(s32[16,512]{1,0:T(8,128)} %bitcast.12, s32[16,512]{1,0:T(8,128)} %bitcast.13, s32[16,512]{1,0:T(8,128)} %bitcast.14, f32[16,512]{1,0:T(8,128)} %bitcast.15, f32[16,512]{1,0:T(8,128)} %bitcast.16, f32[16,512]{1,0:T(8,128)} %bitcast.17, s32[1,512]{1,0:T(1,128)} %bitcast.18, s32[1,512]{1,0:T(1,128)} %bitcast.19, ...), custom_call_target="tpu_custom_call" | custom-call | tf_op jit(solution)/shard_map/pack/pallas_call | solution.py:388
  1.1 15.5 %all_to_all.5.ref = f32[8,56,128]{2,1,0:T(8,128)S(1)} all-to-all(f32[8,56,128]{2,1,0:T(8,128)S(1)} %pack.1), channel_id=1, replica_groups=mesh['book'=2,'trade'=8,'path'=2] {'trade'}, dimensions={0} | all-to-all | bytes 458752 | tf_op jit(solution)/shard_map/all_to_all | solution.py:397
  16.5 2.1 %price.1 = f32[16,32]{1,0:T(8,128)} custom-call(f32[8,56,128]{2,1,0:T(8,128)S(1)} %all_to_all.5.ref), custom_call_target="tpu_custom_call" | custom-call | tf_op jit(solution)/shard_map/price/pallas_call | solution.py:398

commit v3 on v0

--- a/solution.py
+++ b/solution.py
@@ -3,6 +3,8 @@
 import jax
 import jax.numpy as jnp
 from jax import lax
+from jax.experimental import pallas as pl
+from jax.experimental.pallas import tpu as pltpu
 from jax.sharding import PartitionSpec as P
 
 GRID = 128
@@ -166,7 +168,7 @@
     return totals.reshape(block_rows, -1)
 
 
-def shards(
+def shards_by_sum(
     shocks, trade_kind, cash_start, cash_count, strike, normal_vol, notional, block_count, block_set
 ):
     dates_count = shocks.shape[1]
@@ -190,6 +192,289 @@
     return jnp.maximum(netted, 0.0).reshape(SET_DEV, dates_count, -1)
 
 
+SLOTS_TILE = 8
+LANES = 128
+FIELDS = 6
+ROWS = (FIELDS + 1) * SLOTS_TILE
+INPUTS = range(9)
+NEAR = 1
+FAR = ((3, 6), (2, 5), (4, 7))
+DATES = 2
+VMEM_BYTES = 8 * 2**20
+
+TAIL = (
+    -1.325748085975647,
+    -1.8081518411636353,
+    -0.41172587871551514,
+    -0.042724475264549255,
+    0.0027914412785321474,
+    0.00040712140616960824,
+    -0.00013435240543913096,
+    1.5000393432273995e-05,
+    -6.33199476851587e-07,
+)
+
+
+def iota(shape, dimension):
+    return lax.broadcasted_iota(jnp.int32, shape, dimension)
+
+
+def offsets(core):
+    return [NEAR] + [jnp.where(core == 0, first, second) for first, second in FAR]
+
+
+def pack(*refs):
+    count_of = len(INPUTS)
+    sources, outs = refs[:count_of], refs[count_of : count_of + 2 + len(FAR)]
+    grid = refs[count_of + 2 + len(FAR)]
+    held, arrived = refs[count_of + 3 + len(FAR) : -1], refs[-1]
+    copies = [
+        pltpu.make_async_copy(source, target, arrived.at[at])
+        for at, (source, target) in enumerate(zip(sources, held))
+    ]
+    for copy in copies:
+        copy.start()
+    for at, rows in enumerate(curve_rows()):
+        grid[at] = rows
+    me, core = lax.axis_index("trade"), lax.axis_index("path")
+    half = LANES // 2
+    low = iota((SLOTS_TILE, LANES), 1) < half
+    row, lane = iota((SLOTS_TILE, LANES), 0), iota((SLOTS_TILE, LANES), 1)
+    for copy in copies:
+        copy.wait()
+    kind, start, count, strike, vol, notional, live, group, shocks = held
+    own_shocks = jnp.zeros((SLOTS_TILE, LANES), jnp.float32)
+    for factor in range(2):
+        for date in range(DATES):
+            value = jnp.broadcast_to(shocks[factor : factor + 1, date : date + 1], (SLOTS_TILE, LANES))
+            own_shocks = jnp.where(lane == factor * DATES + date, value, own_shocks)
+    for out, offset in zip(outs, [0] + offsets(core)):
+        owner = me ^ offset
+        cut = pl.ds(pl.multiple_of(owner // 2 * LANES, LANES), LANES)
+        odd = owner % 2
+
+        def both(low_half, high_half):
+            return jnp.where(
+                low, pltpu.roll(low_half, half * odd, 1), pltpu.roll(high_half, half * (1 - odd), 1)
+            )
+
+        def field(ref):
+            return both(ref[:SLOTS_TILE, cut], ref[SLOTS_TILE:, cut])
+
+        lives = jnp.broadcast_to(live[:, cut], (SLOTS_TILE, LANES))
+        sets = jnp.broadcast_to(group[:, cut], (SLOTS_TILE, LANES))
+        slot = row + jnp.where(low, 0, SLOTS_TILE)
+        first, kinds = field(start), field(kind)
+        size = jnp.where(kinds == 2, 2.0, 1.0) * field(notional)
+        tiles = (
+            first.astype(jnp.float32),
+            (first + field(count)).astype(jnp.float32),
+            field(strike),
+            field(vol),
+            jnp.where(slot < both(lives, lives), size, 0.0),
+            jnp.where(kinds == 1, 1.0, jnp.where(kinds == 2, 0.5, 0.0)),
+            jnp.where(row == 0, (both(sets, sets) - owner * SET_DEV).astype(jnp.float32), own_shocks),
+        )
+        for at, tile in enumerate(tiles):
+            out[at * SLOTS_TILE : (at + 1) * SLOTS_TILE, :] = tile
+
+
+def add_shocks(shocks, *refs):
+    core = lax.axis_index("path")
+    lane = iota((1, LANES), 1)
+    line = jnp.zeros((1, LANES), jnp.float32)
+    for factor in range(2):
+        for date in range(DATES):
+            value = jnp.broadcast_to(shocks[factor : factor + 1, date : date + 1], (1, LANES))
+            line = jnp.where(lane == factor * DATES + date, value, line)
+    for ref in refs[len(FAR) :]:
+        ref[pl.ds(FIELDS * SLOTS_TILE + 2 - core, 1), :] = line
+
+
+def split(values, count):
+    parts = []
+    for _ in range(count):
+        part = values.astype(jnp.bfloat16)
+        parts.append(part)
+        values = values - part.astype(jnp.float32)
+    return jnp.concatenate(parts, axis=0)
+
+
+def add_parts(product, count):
+    rows = product.shape[0] // count
+    total = product[(count - 1) * rows :]
+    for part in range(count - 2, -1, -1):
+        total = total + product[part * rows : (part + 1) * rows]
+    return total
+
+
+def curve_rows():
+    node = iota((SLOTS_TILE, GRID), 1).astype(jnp.float32) * YEAR_STEP
+    row = iota((SLOTS_TILE, GRID), 0)
+    valued = jnp.where(row < DATES + 1, row, 1).astype(jnp.float32) * YEAR_STEP
+    horizon = node - valued
+    front = -FLAT_RATE * horizon + 0.5 * (
+        factor_variance(horizon) - factor_variance(node) + factor_variance(valued)
+    )
+    return front, loading(REVERT_FAST, horizon), loading(REVERT_SLOW, horizon)
+
+
+def tables(shocks, grid):
+    states = evolve(shocks)
+    discounts = []
+    for date in range(DATES):
+        front, fast, slow = (grid[at, date + 1 : date + 2, :] for at in range(3))
+        discounts.append(jnp.exp(front - fast * states[0, date] - slow * states[1, date]))
+    both = jnp.concatenate(discounts, axis=0)
+    mid = GRID // 4
+    source, target = iota((GRID, GRID), 0), iota((GRID, GRID), 1)
+    weights = jnp.where((source > mid) & (source <= target), YEAR_STEP, 0.0) - jnp.where(
+        (source <= mid) & (source > target), YEAR_STEP, 0.0
+    )
+    sums = jnp.dot(split(both, 3), weights.astype(jnp.bfloat16), preferred_element_type=jnp.float32)
+    return both, add_parts(sums, 3)
+
+
+def price_source(ref, discount, running, masks):
+    def field(at):
+        return ref[at * SLOTS_TILE : (at + 1) * SLOTS_TILE, :]
+
+    def look_up(table, at, index):
+        row = jnp.broadcast_to(table[at : at + 1, :], (SLOTS_TILE, LANES))
+        return jnp.take_along_axis(row, index, axis=1, mode="promise_in_bounds")
+
+    first, last = field(0), field(1)
+    first_node, last_node = first.astype(jnp.int32), last.astype(jnp.int32)
+    strike, vol, size, offset = field(2), field(3), field(4), field(5)
+    tilt = 0.5 - offset
+    totals = []
+    for date in range(DATES):
+        spread = vol * jnp.sqrt(first * YEAR_STEP - (date + 1) * YEAR_STEP)
+        inverse = 1.0 / spread
+        scale = size * spread
+        hurdle = strike * inverse
+        rows = range(date * SLOTS_TILE, (date + 1) * SLOTS_TILE)
+        starts = [(look_up(discount, at, first_node), look_up(running, at, first_node)) for at in rows]
+        ends = [(look_up(discount, at, last_node), look_up(running, at, last_node)) for at in rows]
+        values = []
+        for (curve_start, sum_start), (curve_end, sum_end) in zip(starts, ends):
+            float_leg, annuity = curve_start - curve_end, sum_end - sum_start
+            standard = float_leg * pl.reciprocal(annuity) * inverse - hurdle
+            size_of = jnp.abs(standard)
+            power = jnp.full_like(size_of, TAIL[-1])
+            for term in TAIL[-2::-1]:
+                power = power * size_of + term
+            values.append(scale * annuity * (0.5 * size_of + tilt * standard + jnp.exp2(power)))
+        for bit, mask in zip((1, 2, 4), masks):
+            values = [
+                jnp.where(mask, a, b) + pltpu.roll(jnp.where(mask, b, a), bit, 0)
+                for a, b in zip(values[::2], values[1::2])
+            ]
+        totals.append(values[0])
+    return jnp.concatenate(totals, axis=0)
+
+
+def price(*refs):
+    refs, (grid, out, discount, running) = refs[:-4], refs[-4:]
+    extra = FIELDS * SLOTS_TILE
+    me, core = lax.axis_index("trade"), lax.axis_index("path")
+    row = iota((SLOTS_TILE, LANES), 0)
+    lines = jnp.zeros((SLOTS_TILE, LANES), jnp.float32)
+    for ref, offset in zip(refs, [0] + offsets(core) + offsets(1 - core)[1:]):
+        line = jnp.broadcast_to(ref[pl.ds(extra + 1 + core, 1), :], (SLOTS_TILE, LANES))
+        lines = jnp.where(row == (me ^ offset), line, lines)
+    shocks = jnp.stack(
+        [
+            jnp.stack(
+                [
+                    jnp.broadcast_to(lines[:, at : at + 1], (SLOTS_TILE, LANES))
+                    for at in range(factor * DATES, (factor + 1) * DATES)
+                ]
+            )
+            for factor in range(2)
+        ]
+    )
+    discount[...], running[...] = tables(shocks, grid)
+    masks = [(row & bit) == 0 for bit in (1, 2, 4)]
+    set_index = iota((SET_DEV, LANES), 0).astype(jnp.float32)
+    one_hot = jnp.concatenate(
+        [(set_index == ref[extra : extra + 1, :]).astype(jnp.bfloat16) for ref in refs], axis=1
+    )
+    totals = jnp.concatenate([price_source(ref, discount, running, masks) for ref in refs], axis=1)
+    netted = lax.dot_general(
+        split(totals, 3), one_hot, (((1,), (1,)), ((), ())), preferred_element_type=jnp.float32
+    )
+    out[...] = jnp.maximum(add_parts(netted, 3), 0.0)
+
+
+def shards_by_trade(
+    shocks, trade_kind, cash_start, cash_count, strike, normal_vol, notional, block_count, block_set
+):
+    dates_count = shocks.shape[1]
+    own_shocks = shocks.reshape(2, dates_count)
+    swap = [(0, 1), (1, 0)]
+    other_shocks = lax.ppermute(own_shocks, "path", swap)
+    fields = (
+        trade_kind.T,
+        cash_start.T,
+        cash_count.T,
+        strike.T,
+        normal_vol.T,
+        notional.T,
+        block_count.reshape(1, -1),
+        block_set.reshape(1, -1),
+        own_shocks,
+    )
+    message = jax.ShapeDtypeStruct((ROWS, LANES), jnp.float32)
+    limit = pltpu.CompilerParams(vmem_limit_bytes=VMEM_BYTES)
+    own, near, *far, grid = pl.pallas_call(
+        pack,
+        out_shape=[message] * (2 + len(FAR)) + [jax.ShapeDtypeStruct((3, SLOTS_TILE, GRID), jnp.float32)],
+        in_specs=[pl.BlockSpec(memory_space=pltpu.HBM)] * len(fields),
+        scratch_shapes=[pltpu.VMEM(field.shape, field.dtype) for field in fields]
+        + [pltpu.SemaphoreType.DMA((len(fields),))],
+        compiler_params=limit,
+        name="pack",
+    )(*(pltpu.with_memory_space_constraint(field, pltpu.HBM) for field in fields))
+    owners = lax.axis_size("trade")
+    near_in = lax.ppermute(near, "trade", [(at, at ^ NEAR) for at in range(owners)])
+    far = pl.pallas_call(
+        add_shocks,
+        out_shape=[message] * len(FAR),
+        input_output_aliases={1 + at: at for at in range(len(FAR))},
+        compiler_params=limit,
+        name="add_shocks",
+    )(other_shocks, *far)
+    far_in = []
+    for piece, pair in zip(far, FAR):
+        turns = [(2 * at + core, 2 * (at ^ pair[core]) + core) for at in range(owners) for core in range(2)]
+        far_in.append(lax.ppermute(piece, ("trade", "path"), turns))
+    handed = [lax.ppermute(piece, "path", swap) for piece in far_in]
+    netted = pl.pallas_call(
+        price,
+        out_shape=jax.ShapeDtypeStruct((dates_count * SLOTS_TILE, SET_DEV), jnp.float32),
+        scratch_shapes=[
+            pltpu.VMEM((dates_count * SLOTS_TILE, GRID), jnp.float32),
+            pltpu.VMEM((dates_count * SLOTS_TILE, GRID), jnp.float32),
+        ],
+        compiler_params=limit,
+        name="price",
+    )(own, near_in, *far_in, *handed, grid)
+    return netted.reshape(dates_count, SLOTS_TILE, SET_DEV).transpose(2, 0, 1)
+
+
+def shards(shocks, trade_kind, *others):
+    blocks, slot_count = trade_kind.shape
+    by_trade = (
+        lax.axis_size("trade") == SLOTS_TILE
+        and lax.axis_size("path") == 2
+        and shocks.shape == (2, DATES, 1, 1)
+        and slot_count == 2 * SLOTS_TILE
+        and blocks == SLOTS_TILE * LANES // 2
+    )
+    return (shards_by_trade if by_trade else shards_by_sum)(shocks, trade_kind, *others)
+
+
 def solution(mesh):
     placed = (
         P("book", None, "path", "trade"),

time: 136 us -> 15.5 us (0.11)
  waiting for transfers between devices: 58.3 us -> 0.86 us
  blocking collectives: 22.2 us -> 0 us
  between operations: 17.7 us -> 0.03 us
  other arithmetic: 12.5 us -> 0 us
  local copies, waits for them, and re-layouts: 13.1 us -> 0.68 us
  starting transfers between devices: 0.01 us -> 10.8 us
  matrix products: 9.83 us -> 0 us
  Pallas kernels: 0 us -> 2.9 us
  loops' own time: 1.92 us -> 0 us
    unnamed x2 -> x0, waiting for transfers between devices: 58.3 us -> none
    all_gather x1 -> x0, blocking collectives: 22.2 us -> none  [shards(): gathered = lax.all_gather(own_states, 'trade', axis=2, tiled=True)]
    ppermute x0 -> x8, starting transfers between devices: none -> 10.8 us  [the longest x3 6.57 us: shards_by_trade(): far_in.append(lax.ppermute(piece, ('trade', 'path'), turns))]
    dot_general x16 -> x0, matrix products: 8.83 us -> none  [price_blocks(): jnp.dot(weights, discounts, precision=HIGHEST, preferred_element_type=jnp...]
    unnamed x25 -> x2, local copies, waits for them, and re-layouts: 6.46 us -> 0.68 us
    reduce_sum x16 -> x0, other arithmetic: 4.3 us -> none  [price_blocks(): return jnp.sum(trade_value, axis=1).reshape(groups, -1)]
    squeeze x32 -> x0, local copies, waits for them, and re-layouts: 3.88 us -> none  [the longest x16 1.95 us: price_blocks(): float_leg = products[1]]
    select_n x32 -> x0, other arithmetic: 3.43 us -> none  [the longest x16 3.23 us: price_blocks(): jnp.where((cash_nodes > first_node) & (cash_nodes <= last_node), YEAR_STE...]
  transfers between devices with their start and end apart: 1 -> 8, of which waited for: 1 -> 2; matrix products, arithmetic and copies ran while one was open for 0% -> 0% of each run, Pallas kernels for 0% -> 7%
where the time goes in v3:
time: 15.5 us; the launch traced here: 15.3 us
  starting transfers between devices  10.8 us (70%)
  Pallas kernels  2.9 us (19%)
  waiting for transfers between devices  0.86 us (6%)
  local copies, waits for them, and re-layouts  0.68 us (4%)
    ppermute x3, starting transfers between devices, shards_by_trade(): far_in.append(lax.ppermute(piece, ('trade', 'path'), turns))  6.57 us
    ppermute x3, starting transfers between devices, shards_by_trade(): handed = [lax.ppermute(piece, 'path', swap) for piece in far_in]  3.26 us
    pallas_call x1, Pallas kernels, shards_by_trade(): pl.pallas_call(price, out_shape=jax.ShapeDtypeStruct((dates_count * SLOTS...  1.73 us
    pallas_call x1, Pallas kernels, shards_by_trade(): pl.pallas_call(pack, out_shape=[message] * (2 + len(FAR)) + [jax.ShapeDty...  1.09 us
    unnamed x2, local copies, waits for them, and re-layouts  0.68 us
    ppermute x1, starting transfers between devices, shards_by_trade(): lax.ppermute(near, 'trade', [(at, at ^ NEAR) for at in range(owners)])  0.54 us
    ppermute x3, waiting for transfers between devices, shards_by_trade(): handed = [lax.ppermute(piece, 'path', swap) for piece in far_in]  0.48 us
    ppermute x1, starting transfers between devices, shards_by_trade(): other_shocks = lax.ppermute(own_shocks, 'path', swap)  0.45 us
  transfers between devices with their start and end apart: 8, of which 2 were waited for; matrix products, arithmetic and copies ran while one was open for 0% of the time, Pallas kernels for 7%

profile of v3, /device:TPU:0, one launch (start us, length us, event | category | flops | bytes accessed | tf_op | source)
XLA Modules:
  0.0 15.3 jit_solution(7113117136924577072)
XLA Ops:
  0.0 0.0 copy-start
  0.0 0.7 %copy-done = f32[2,2,1,1]{1,3,2,0:T(1,128)S(1)} copy-done((f32[2,2,1,1]{1,3,2,0:T(1,128)S(1)}, f32[2,2,1,1]{1,3,2,0:T(1,128)}, u32[]{:S(2)}) %copy-start) | copy-done | bytes 40
  0.7 0.5 %collective-permute-start.1 = (f32[2,2]{1,0:T(2,128)S(1)}, f32[2,2]{1,0:T(2,128)S(1)}, u32[]{:S(2)}, u32[]{:S(2)}) collective-permute-start(f32[2,2]{1,0:T(2,128)S(1)} %bitcast.21), channel_id=1, source_target_pairs={{0,1},{1,0},{2,3},{3,2},{4,5},{5,4},{6,7},{7,6},{8,9},{9,8},{10,11... | collective-permute-start | bytes 56 | tf_op jit(solution)/shard_map/ppermute | solution.py:416
  1.1 1.1 %pack.1 = (f32[56,128]{1,0:T(8,128)S(1)}, f32[56,128]{1,0:T(8,128)S(1)}, f32[56,128]{1,0:T(8,128)S(1)}, f32[56,128]{1,0:T(8,128)S(1)}, f32[56,128]{1,0:T(8,128)S(1)}, /*index=5*/f32[3,8,128]{2,1,0:T(8,128)S(1)}) custom-call(s32[16,512]{1,0:T(8,128)} %bitcast.12, s32[16,512]{1,0:T(8,128)} %bitcast.13, s32[16,512]{1,0:T(8,128)} %bitcast.14, ...), custom_call_target="tpu_custom_call" | custom-call | tf_op jit(solution)/shard_map/pack/pallas_call | solution.py:430
  2.2 0.0 collective-permute-done.1.shocks
  2.2 0.1 add_shocks.1
  2.3 3.5 %collective-permute-start.2 = (f32[56,128]{1,0:T(8,128)S(1)}, f32[56,128]{1,0:T(8,128)S(1)}, u32[]{:S(2)}, u32[]{:S(2)}) collective-permute-start(f32[56,128]{1,0:T(8,128)S(1)} %get-tuple-element.19), channel_id=1, source_target_pairs={{0,6},{1,13},{2,4},{3,15},{4,2},{5,9},{6,0},{7,11},{8,14},{9,5},{1... | collective-permute-start | bytes 86024 | tf_op jit(solution)/shard_map/ppermute | solution.py:451
  5.8 0.4 %collective-permute-start.3 = (f32[56,128]{1,0:T(8,128)S(1)}, f32[56,128]{1,0:T(8,128)S(1)}, u32[]{:S(2)}, u32[]{:S(2)}) collective-permute-start(f32[56,128]{1,0:T(8,128)S(1)} %get-tuple-element.20), channel_id=1, source_target_pairs={{0,4},{1,11},{2,6},{3,9},{4,0},{5,15},{6,2},{7,13},{8,12},{9,3},{1... | collective-permute-start | bytes 86024 | tf_op jit(solution)/shard_map/ppermute | solution.py:451
  6.3 2.6 %collective-permute-start.4 = (f32[56,128]{1,0:T(8,128)S(1)}, f32[56,128]{1,0:T(8,128)S(1)}, u32[]{:S(2)}, u32[]{:S(2)}) collective-permute-start(f32[56,128]{1,0:T(8,128)S(1)} %get-tuple-element.21), channel_id=1, source_target_pairs={{0,8},{1,15},{2,10},{3,13},{4,12},{5,11},{6,14},{7,9},{8,0},{9,7},... | collective-permute-start | bytes 86024 | tf_op jit(solution)/shard_map/ppermute | solution.py:451
  8.9 0.5 %collective-permute-start = (f32[56,128]{1,0:T(8,128)S(1)}, f32[56,128]{1,0:T(8,128)S(1)}, u32[]{:S(2)}, u32[]{:S(2)}) collective-permute-start(f32[56,128]{1,0:T(8,128)S(1)} %get-tuple-element.15), channel_id=1, source_target_pairs={{0,2},{2,0},{4,6},{6,4},{8,10},{10,8},{12,14},{14,12},{1,3},{3,1},... | collective-permute-start | bytes 86024 | tf_op jit(solution)/shard_map/ppermute | solution.py:440
  9.4 0.0 collective-permute-done.2.refs_2_
  9.4 1.2 %collective-permute-start.5 = (f32[56,128]{1,0:T(8,128)S(1)}, f32[56,128]{1,0:T(8,128)S(1)}, u32[]{:S(2)}, u32[]{:S(2)}) collective-permute-start(f32[56,128]{1,0:T(8,128)S(1)} %collective-permute-done.2.refs_2_), channel_id=1, source_target_pairs={{0,1},{1,0},{2,3},{3,2},{4,5},{5,4},{6,7},{7,6},{8,9},{9,8},{10,11... | collective-permute-start | bytes 86024 | tf_op jit(solution)/shard_map/ppermute | solution.py:452
  10.6 0.0 collective-permute-done.3.refs_3_
  10.6 1.4 %collective-permute-start.6 = (f32[56,128]{1,0:T(8,128)S(1)}, f32[56,128]{1,0:T(8,128)S(1)}, u32[]{:S(2)}, u32[]{:S(2)}) collective-permute-start(f32[56,128]{1,0:T(8,128)S(1)} %collective-permute-done.3.refs_3_), channel_id=1, source_target_pairs={{0,1},{1,0},{2,3},{3,2},{4,5},{5,4},{6,7},{7,6},{8,9},{9,8},{10,11... | collective-permute-start | bytes 86024 | tf_op jit(solution)/shard_map/ppermute | solution.py:452
  12.0 0.0 collective-permute-done.4.refs_4_
  12.0 0.7 %collective-permute-start.7 = (f32[56,128]{1,0:T(8,128)S(1)}, f32[56,128]{1,0:T(8,128)S(1)}, u32[]{:S(2)}, u32[]{:S(2)}) collective-permute-start(f32[56,128]{1,0:T(8,128)S(1)} %collective-permute-done.4.refs_4_), channel_id=1, source_target_pairs={{0,1},{1,0},{2,3},{3,2},{4,5},{5,4},{6,7},{7,6},{8,9},{9,8},{10,11... | collective-permute-start | bytes 86024 | tf_op jit(solution)/shard_map/ppermute | solution.py:452
  12.7 0.4 %collective-permute-done.refs_1_ = f32[56,128]{1,0:T(8,128)S(1)} collective-permute-done((f32[56,128]{1,0:T(8,128)S(1)}, f32[56,128]{1,0:T(8,128)S(1)}, u32[]{:S(2)}, u32[]{:S(2)}) %collective-permute-start) | collective-permute-done | bytes 28704 | tf_op jit(solution)/shard_map/ppermute | solution.py:440
  13.1 0.0 collective-permute-done.5.refs_5_
  13.1 0.0 collective-permute-done.6.refs_6_
  13.1 0.5 %collective-permute-done.7.refs_7_ = f32[56,128]{1,0:T(8,128)S(1)} collective-permute-done((f32[56,128]{1,0:T(8,128)S(1)}, f32[56,128]{1,0:T(8,128)S(1)}, u32[]{:S(2)}, u32[]{:S(2)}) %collective-permute-start.7) | collective-permute-done | bytes 28704 | tf_op jit(solution)/shard_map/ppermute | solution.py:452
  13.6 1.7 %price.1 = f32[16,32]{1,0:T(8,128)} custom-call(f32[56,128]{1,0:T(8,128)S(1)} %get-tuple-element.14.refs_0_, f32[56,128]{1,0:T(8,128)S(1)} %collective-permute-done.refs_1_, f32[56,128]{1,0:T(8,128)S(1)} %collective-permute-done.2.refs_2_, f32[56,128]{1,0:T(8,128)S(1)} %collective-permute-done.3.refs_3_, f32[56,128]{1,0:T(8,128)S(1)} %collective-permute-done.4.refs_4_, ...), custom_call_target="tpu_custom_call" | custom-call | tf_op jit(solution)/shard_map/price/pallas_call | solution.py:453
Async XLA Ops:
  0.0 0.7 %copy-start = (f32[2,2,1,1]{1,3,2,0:T(1,128)S(1)}, f32[2,2,1,1]{1,3,2,0:T(1,128)}, u32[]{:S(2)}) copy-start(f32[2,2,1,1]{1,3,2,0:T(1,128)} %param.9) | copy-start | bytes 52
  0.7 1.6 %collective-permute-start.1 = (f32[2,2]{1,0:T(2,128)S(1)}, f32[2,2]{1,0:T(2,128)S(1)}, u32[]{:S(2)}, u32[]{:S(2)}) collective-permute-start(f32[2,2]{1,0:T(2,128)S(1)} %bitcast.21), channel_id=1, source_target_pairs={{0,1},{1,0},{2,3},{3,2},{4,5},{5,4},{6,7},{7,6},{8,9},{9,8},{10,11... | collective-permute-start | bytes 56 | tf_op jit(solution)/shard_map/ppermute | solution.py:416
  2.3 7.1 %collective-permute-start.2 = (f32[56,128]{1,0:T(8,128)S(1)}, f32[56,128]{1,0:T(8,128)S(1)}, u32[]{:S(2)}, u32[]{:S(2)}) collective-permute-start(f32[56,128]{1,0:T(8,128)S(1)} %get-tuple-element.19), channel_id=1, source_target_pairs={{0,6},{1,13},{2,4},{3,15},{4,2},{5,9},{6,0},{7,11},{8,14},{9,5},{1... | collective-permute-start | bytes 86024 | tf_op jit(solution)/shard_map/ppermute | solution.py:451
  5.8 4.8 %collective-permute-start.3 = (f32[56,128]{1,0:T(8,128)S(1)}, f32[56,128]{1,0:T(8,128)S(1)}, u32[]{:S(2)}, u32[]{:S(2)}) collective-permute-start(f32[56,128]{1,0:T(8,128)S(1)} %get-tuple-element.20), channel_id=1, source_target_pairs={{0,4},{1,11},{2,6},{3,9},{4,0},{5,15},{6,2},{7,13},{8,12},{9,3},{1... | collective-permute-start | bytes 86024 | tf_op jit(solution)/shard_map/ppermute | solution.py:451
  6.3 5.7 %collective-permute-start.4 = (f32[56,128]{1,0:T(8,128)S(1)}, f32[56,128]{1,0:T(8,128)S(1)}, u32[]{:S(2)}, u32[]{:S(2)}) collective-permute-start(f32[56,128]{1,0:T(8,128)S(1)} %get-tuple-element.21), channel_id=1, source_target_pairs={{0,8},{1,15},{2,10},{3,13},{4,12},{5,11},{6,14},{7,9},{8,0},{9,7},... | collective-permute-start | bytes 86024 | tf_op jit(solution)/shard_map/ppermute | solution.py:451
  8.9 4.2 %collective-permute-start = (f32[56,128]{1,0:T(8,128)S(1)}, f32[56,128]{1,0:T(8,128)S(1)}, u32[]{:S(2)}, u32[]{:S(2)}) collective-permute-start(f32[56,128]{1,0:T(8,128)S(1)} %get-tuple-element.15), channel_id=1, source_target_pairs={{0,2},{2,0},{4,6},{6,4},{8,10},{10,8},{12,14},{14,12},{1,3},{3,1},... | collective-permute-start | bytes 86024 | tf_op jit(solution)/shard_map/ppermute | solution.py:440
  9.4 3.6 %collective-permute-start.5 = (f32[56,128]{1,0:T(8,128)S(1)}, f32[56,128]{1,0:T(8,128)S(1)}, u32[]{:S(2)}, u32[]{:S(2)}) collective-permute-start(f32[56,128]{1,0:T(8,128)S(1)} %collective-permute-done.2.refs_2_), channel_id=1, source_target_pairs={{0,1},{1,0},{2,3},{3,2},{4,5},{5,4},{6,7},{7,6},{8,9},{9,8},{10,11... | collective-permute-start | bytes 86024 | tf_op jit(solution)/shard_map/ppermute | solution.py:452
  10.6 2.4 %collective-permute-start.6 = (f32[56,128]{1,0:T(8,128)S(1)}, f32[56,128]{1,0:T(8,128)S(1)}, u32[]{:S(2)}, u32[]{:S(2)}) collective-permute-start(f32[56,128]{1,0:T(8,128)S(1)} %collective-permute-done.3.refs_3_), channel_id=1, source_target_pairs={{0,1},{1,0},{2,3},{3,2},{4,5},{5,4},{6,7},{7,6},{8,9},{9,8},{10,11... | collective-permute-start | bytes 86024 | tf_op jit(solution)/shard_map/ppermute | solution.py:452
  12.0 1.6 %collective-permute-start.7 = (f32[56,128]{1,0:T(8,128)S(1)}, f32[56,128]{1,0:T(8,128)S(1)}, u32[]{:S(2)}, u32[]{:S(2)}) collective-permute-start(f32[56,128]{1,0:T(8,128)S(1)} %collective-permute-done.4.refs_4_), channel_id=1, source_target_pairs={{0,1},{1,0},{2,3},{3,2},{4,5},{5,4},{6,7},{7,6},{8,9},{9,8},{10,11... | collective-permute-start | bytes 86024 | tf_op jit(solution)/shard_map/ppermute | solution.py:452

commit v4 on v3

--- a/solution.py
+++ b/solution.py
@@ -198,7 +198,7 @@
 ROWS = (FIELDS + 1) * SLOTS_TILE
 INPUTS = range(9)
 NEAR = 1
-FAR = ((3, 6), (2, 5), (4, 7))
+FAR = ((2, 4), (3, 6), (5, 7))
 DATES = 2
 VMEM_BYTES = 8 * 2**20
 
@@ -413,7 +413,7 @@
     dates_count = shocks.shape[1]
     own_shocks = shocks.reshape(2, dates_count)
     swap = [(0, 1), (1, 0)]
-    other_shocks = lax.ppermute(own_shocks, "path", swap)
+    other_shocks = lax.ppermute(shocks, "path", swap).reshape(2, dates_count)
     fields = (
         trade_kind.T,
         cash_start.T,

time: 15.5 us -> 14.8 us (0.955)
  starting transfers between devices: 10.8 us -> 9.67 us
  waiting for transfers between devices: 0.86 us -> 1.98 us
  local copies, waits for them, and re-layouts: 0.68 us -> 0 us
    ppermute x3, starting transfers between devices: 3.26 us -> 0.98 us  [shards_by_trade(): handed = [lax.ppermute(piece, 'path', swap) for piece in far_in]]
    ppermute x3, waiting for transfers between devices: 0.01 us -> 1.13 us  [shards_by_trade(): far_in.append(lax.ppermute(piece, ('trade', 'path'), turns))]
    ppermute x1, starting transfers between devices: 0.54 us -> 1.49 us  [shards_by_trade(): lax.ppermute(near, 'trade', [(at, at ^ NEAR) for at in range(owners)])]
    unnamed x2 -> x0, local copies, waits for them, and re-layouts: 0.68 us -> none
    ppermute x1, waiting for transfers between devices: 0.37 us -> 0.68 us  [shards_by_trade(): lax.ppermute(near, 'trade', [(at, at ^ NEAR) for at in range(owners)])]
    ppermute x3, waiting for transfers between devices: 0.48 us -> 0.18 us  [shards_by_trade(): handed = [lax.ppermute(piece, 'path', swap) for piece in far_in]]
    ppermute x3, starting transfers between devices: 6.57 us -> 6.75 us  [shards_by_trade(): far_in.append(lax.ppermute(piece, ('trade', 'path'), turns))]
  transfers between devices with their start and end apart: 8 -> 8, of which waited for: 2 -> 3; matrix products, arithmetic and copies ran while one was open for 0% -> 0% of each run, Pallas kernels for 7% -> 7%
where the time goes in v4:
time: 14.8 us; the launch traced here: 14.6 us
  starting transfers between devices  9.67 us (65%)
  Pallas kernels  2.9 us (20%)
  waiting for transfers between devices  1.98 us (13%)
    ppermute x3, starting transfers between devices, shards_by_trade(): far_in.append(lax.ppermute(piece, ('trade', 'path'), turns))  6.75 us
    pallas_call x1, Pallas kernels, shards_by_trade(): pl.pallas_call(price, out_shape=jax.ShapeDtypeStruct((dates_count * SLOTS...  1.73 us
    ppermute x1, starting transfers between devices, shards_by_trade(): lax.ppermute(near, 'trade', [(at, at ^ NEAR) for at in range(owners)])  1.49 us
    ppermute x3, waiting for transfers between devices, shards_by_trade(): far_in.append(lax.ppermute(piece, ('trade', 'path'), turns))  1.13 us
    pallas_call x1, Pallas kernels, shards_by_trade(): pl.pallas_call(pack, out_shape=[message] * (2 + len(FAR)) + [jax.ShapeDty...  1.09 us
    ppermute x3, starting transfers between devices, shards_by_trade(): handed = [lax.ppermute(piece, 'path', swap) for piece in far_in]  0.98 us
    ppermute x1, waiting for transfers between devices, shards_by_trade(): lax.ppermute(near, 'trade', [(at, at ^ NEAR) for at in range(owners)])  0.68 us
    ppermute x1, starting transfers between devices, shards_by_trade(): other_shocks = lax.ppermute(shocks, 'path', swap).reshape(2, dates_count)  0.45 us
  transfers between devices with their start and end apart: 8, of which 3 were waited for; matrix products, arithmetic and copies ran while one was open for 0% of the time, Pallas kernels for 7%

profile of v4, /device:TPU:0, one launch (start us, length us, event | category | flops | bytes accessed | tf_op | source)
XLA Modules:
  0.0 14.6 jit_solution(15088634395036829593)
XLA Ops:
  0.0 0.5 %collective-permute-start.1 = (f32[2,2,1,1]{1,3,2,0:T(1,128)}, f32[2,2,1,1]{1,3,2,0:T(1,128)S(1)}, u32[]{:S(2)}, u32[]{:S(2)}) collective-permute-start(f32[2,2,1,1]{1,3,2,0:T(1,128)} %param.9), channel_id=1, source_target_pairs={{0,1},{1,0},{2,3},{3,2},{4,5},{5,4},{6,7},{7,6},{8,9},{9,8},{10,11... | collective-permute-start | bytes 56 | tf_op jit(solution)/shard_map/ppermute | solution.py:416
  0.5 1.1 %pack.1 = (f32[56,128]{1,0:T(8,128)S(1)}, f32[56,128]{1,0:T(8,128)S(1)}, f32[56,128]{1,0:T(8,128)S(1)}, f32[56,128]{1,0:T(8,128)S(1)}, f32[56,128]{1,0:T(8,128)S(1)}, /*index=5*/f32[3,8,128]{2,1,0:T(8,128)S(1)}) custom-call(s32[16,512]{1,0:T(8,128)} %bitcast.14, s32[16,512]{1,0:T(8,128)} %bitcast.15, s32[16,512]{1,0:T(8,128)} %bitcast.16, ...), custom_call_target="tpu_custom_call" | custom-call | tf_op jit(solution)/shard_map/pack/pallas_call | solution.py:430
  1.6 0.0 collective-permute-done.1
  1.6 0.1 add_shocks.1
  1.6 2.8 %collective-permute-start.2 = (f32[56,128]{1,0:T(8,128)S(1)}, f32[56,128]{1,0:T(8,128)S(1)}, u32[]{:S(2)}, u32[]{:S(2)}) collective-permute-start(f32[56,128]{1,0:T(8,128)S(1)} %get-tuple-element.19), channel_id=1, source_target_pairs={{0,4},{1,9},{2,6},{3,11},{4,0},{5,13},{6,2},{7,15},{8,12},{9,1},{1... | collective-permute-start | bytes 86024 | tf_op jit(solution)/shard_map/ppermute | solution.py:451
  4.5 1.4 %collective-permute-start.3 = (f32[56,128]{1,0:T(8,128)S(1)}, f32[56,128]{1,0:T(8,128)S(1)}, u32[]{:S(2)}, u32[]{:S(2)}) collective-permute-start(f32[56,128]{1,0:T(8,128)S(1)} %get-tuple-element.20), channel_id=1, source_target_pairs={{0,6},{1,13},{2,4},{3,15},{4,2},{5,9},{6,0},{7,11},{8,14},{9,5},{1... | collective-permute-start | bytes 86024 | tf_op jit(solution)/shard_map/ppermute | solution.py:451
  5.8 2.6 %collective-permute-start.4 = (f32[56,128]{1,0:T(8,128)S(1)}, f32[56,128]{1,0:T(8,128)S(1)}, u32[]{:S(2)}, u32[]{:S(2)}) collective-permute-start(f32[56,128]{1,0:T(8,128)S(1)} %get-tuple-element.21), channel_id=1, source_target_pairs={{0,10},{1,15},{2,8},{3,13},{4,14},{5,11},{6,12},{7,9},{8,2},{9,7},... | collective-permute-start | bytes 86024 | tf_op jit(solution)/shard_map/ppermute | solution.py:451
  8.4 1.5 %collective-permute-start = (f32[56,128]{1,0:T(8,128)S(1)}, f32[56,128]{1,0:T(8,128)S(1)}, u32[]{:S(2)}, u32[]{:S(2)}) collective-permute-start(f32[56,128]{1,0:T(8,128)S(1)} %get-tuple-element.15), channel_id=1, source_target_pairs={{0,2},{2,0},{4,6},{6,4},{8,10},{10,8},{12,14},{14,12},{1,3},{3,1},... | collective-permute-start | bytes 86024 | tf_op jit(solution)/shard_map/ppermute | solution.py:440
  9.9 0.0 collective-permute-done.2.refs_2_
  9.9 0.0 collective-permute-start.5
  9.9 0.0 collective-permute-done.3.refs_3_
  9.9 0.5 %collective-permute-start.6 = (f32[56,128]{1,0:T(8,128)S(1)}, f32[56,128]{1,0:T(8,128)S(1)}, u32[]{:S(2)}, u32[]{:S(2)}) collective-permute-start(f32[56,128]{1,0:T(8,128)S(1)} %collective-permute-done.3.refs_3_), channel_id=1, source_target_pairs={{0,1},{1,0},{2,3},{3,2},{4,5},{5,4},{6,7},{7,6},{8,9},{9,8},{10,11... | collective-permute-start | bytes 86024 | tf_op jit(solution)/shard_map/ppermute | solution.py:452
  10.4 1.1 %collective-permute-done.4.refs_4_ = f32[56,128]{1,0:T(8,128)S(1)} collective-permute-done((f32[56,128]{1,0:T(8,128)S(1)}, f32[56,128]{1,0:T(8,128)S(1)}, u32[]{:S(2)}, u32[]{:S(2)}) %collective-permute-start.4) | collective-permute-done | bytes 28704 | tf_op jit(solution)/shard_map/ppermute | solution.py:451
  11.5 0.5 %collective-permute-start.7 = (f32[56,128]{1,0:T(8,128)S(1)}, f32[56,128]{1,0:T(8,128)S(1)}, u32[]{:S(2)}, u32[]{:S(2)}) collective-permute-start(f32[56,128]{1,0:T(8,128)S(1)} %collective-permute-done.4.refs_4_), channel_id=1, source_target_pairs={{0,1},{1,0},{2,3},{3,2},{4,5},{5,4},{6,7},{7,6},{8,9},{9,8},{10,11... | collective-permute-start | bytes 86024 | tf_op jit(solution)/shard_map/ppermute | solution.py:452
  12.0 0.7 %collective-permute-done.refs_1_ = f32[56,128]{1,0:T(8,128)S(1)} collective-permute-done((f32[56,128]{1,0:T(8,128)S(1)}, f32[56,128]{1,0:T(8,128)S(1)}, u32[]{:S(2)}, u32[]{:S(2)}) %collective-permute-start) | collective-permute-done | bytes 28704 | tf_op jit(solution)/shard_map/ppermute | solution.py:440
  12.7 0.0 collective-permute-done.5.refs_5_
  12.7 0.0 collective-permute-done.6.refs_6_
  12.7 0.2 %collective-permute-done.7.refs_7_ = f32[56,128]{1,0:T(8,128)S(1)} collective-permute-done((f32[56,128]{1,0:T(8,128)S(1)}, f32[56,128]{1,0:T(8,128)S(1)}, u32[]{:S(2)}, u32[]{:S(2)}) %collective-permute-start.7) | collective-permute-done | bytes 28704 | tf_op jit(solution)/shard_map/ppermute | solution.py:452
  12.8 1.7 %price.1 = f32[16,32]{1,0:T(8,128)} custom-call(f32[56,128]{1,0:T(8,128)S(1)} %get-tuple-element.14.refs_0_, f32[56,128]{1,0:T(8,128)S(1)} %collective-permute-done.refs_1_, f32[56,128]{1,0:T(8,128)S(1)} %collective-permute-done.2.refs_2_, f32[56,128]{1,0:T(8,128)S(1)} %collective-permute-done.3.refs_3_, f32[56,128]{1,0:T(8,128)S(1)} %collective-permute-done.4.refs_4_, ...), custom_call_target="tpu_custom_call" | custom-call | tf_op jit(solution)/shard_map/price/pallas_call | solution.py:453
Async XLA Ops:
  0.0 1.6 %collective-permute-start.1 = (f32[2,2,1,1]{1,3,2,0:T(1,128)}, f32[2,2,1,1]{1,3,2,0:T(1,128)S(1)}, u32[]{:S(2)}, u32[]{:S(2)}) collective-permute-start(f32[2,2,1,1]{1,3,2,0:T(1,128)} %param.9), channel_id=1, source_target_pairs={{0,1},{1,0},{2,3},{3,2},{4,5},{5,4},{6,7},{7,6},{8,9},{9,8},{10,11... | collective-permute-start | bytes 56 | tf_op jit(solution)/shard_map/ppermute | solution.py:416
  1.6 8.2 %collective-permute-start.2 = (f32[56,128]{1,0:T(8,128)S(1)}, f32[56,128]{1,0:T(8,128)S(1)}, u32[]{:S(2)}, u32[]{:S(2)}) collective-permute-start(f32[56,128]{1,0:T(8,128)S(1)} %get-tuple-element.19), channel_id=1, source_target_pairs={{0,4},{1,9},{2,6},{3,11},{4,0},{5,13},{6,2},{7,15},{8,12},{9,1},{1... | collective-permute-start | bytes 86024 | tf_op jit(solution)/shard_map/ppermute | solution.py:451
  4.5 5.5 %collective-permute-start.3 = (f32[56,128]{1,0:T(8,128)S(1)}, f32[56,128]{1,0:T(8,128)S(1)}, u32[]{:S(2)}, u32[]{:S(2)}) collective-permute-start(f32[56,128]{1,0:T(8,128)S(1)} %get-tuple-element.20), channel_id=1, source_target_pairs={{0,6},{1,13},{2,4},{3,15},{4,2},{5,9},{6,0},{7,11},{8,14},{9,5},{1... | collective-permute-start | bytes 86024 | tf_op jit(solution)/shard_map/ppermute | solution.py:451
  5.8 5.7 %collective-permute-start.4 = (f32[56,128]{1,0:T(8,128)S(1)}, f32[56,128]{1,0:T(8,128)S(1)}, u32[]{:S(2)}, u32[]{:S(2)}) collective-permute-start(f32[56,128]{1,0:T(8,128)S(1)} %get-tuple-element.21), channel_id=1, source_target_pairs={{0,10},{1,15},{2,8},{3,13},{4,14},{5,11},{6,12},{7,9},{8,2},{9,7},... | collective-permute-start | bytes 86024 | tf_op jit(solution)/shard_map/ppermute | solution.py:451
  8.4 4.3 %collective-permute-start = (f32[56,128]{1,0:T(8,128)S(1)}, f32[56,128]{1,0:T(8,128)S(1)}, u32[]{:S(2)}, u32[]{:S(2)}) collective-permute-start(f32[56,128]{1,0:T(8,128)S(1)} %get-tuple-element.15), channel_id=1, source_target_pairs={{0,2},{2,0},{4,6},{6,4},{8,10},{10,8},{12,14},{14,12},{1,3},{3,1},... | collective-permute-start | bytes 86024 | tf_op jit(solution)/shard_map/ppermute | solution.py:440
  9.9 2.8 %collective-permute-start.5 = (f32[56,128]{1,0:T(8,128)S(1)}, f32[56,128]{1,0:T(8,128)S(1)}, u32[]{:S(2)}, u32[]{:S(2)}) collective-permute-start(f32[56,128]{1,0:T(8,128)S(1)} %collective-permute-done.2.refs_2_), channel_id=1, source_target_pairs={{0,1},{1,0},{2,3},{3,2},{4,5},{5,4},{6,7},{7,6},{8,9},{9,8},{10,11... | collective-permute-start | bytes 86024 | tf_op jit(solution)/shard_map/ppermute | solution.py:452
  9.9 2.8 %collective-permute-start.6 = (f32[56,128]{1,0:T(8,128)S(1)}, f32[56,128]{1,0:T(8,128)S(1)}, u32[]{:S(2)}, u32[]{:S(2)}) collective-permute-start(f32[56,128]{1,0:T(8,128)S(1)} %collective-permute-done.3.refs_3_), channel_id=1, source_target_pairs={{0,1},{1,0},{2,3},{3,2},{4,5},{5,4},{6,7},{7,6},{8,9},{9,8},{10,11... | collective-permute-start | bytes 86024 | tf_op jit(solution)/shard_map/ppermute | solution.py:452
  11.5 1.3 %collective-permute-start.7 = (f32[56,128]{1,0:T(8,128)S(1)}, f32[56,128]{1,0:T(8,128)S(1)}, u32[]{:S(2)}, u32[]{:S(2)}) collective-permute-start(f32[56,128]{1,0:T(8,128)S(1)} %collective-permute-done.4.refs_4_), channel_id=1, source_target_pairs={{0,1},{1,0},{2,3},{3,2},{4,5},{5,4},{6,7},{7,6},{8,9},{9,8},{10,11... | collective-permute-start | bytes 86024 | tf_op jit(solution)/shard_map/ppermute | solution.py:452

commit v5 on v4

--- a/solution.py
+++ b/solution.py
@@ -199,6 +199,8 @@
 INPUTS = range(9)
 NEAR = 1
 FAR = ((2, 4), (3, 6), (5, 7))
+SLOTS = 8
+EARLY = 6
 DATES = 2
 VMEM_BYTES = 8 * 2**20
 
@@ -221,6 +223,12 @@
 
 def offsets(core):
     return [NEAR] + [jnp.where(core == 0, first, second) for first, second in FAR]
+
+
+def slot_offsets(core):
+    near, *far = offsets(core)
+    *handed, last = offsets(1 - core)[1:]
+    return [0, *far, *handed, near, last]
 
 
 def pack(*refs):
@@ -277,6 +285,7 @@
         )
         for at, tile in enumerate(tiles):
             out[at * SLOTS_TILE : (at + 1) * SLOTS_TILE, :] = tile
+    outs[1][ROWS:, :] = jnp.zeros((SLOTS_TILE, LANES), jnp.float32)
 
 
 def add_shocks(shocks, *refs):
@@ -335,13 +344,22 @@
     return both, add_parts(sums, 3)
 
 
-def price_source(ref, discount, running, masks):
+def price_source(ref, discount, running, slots):
     def field(at):
         return ref[at * SLOTS_TILE : (at + 1) * SLOTS_TILE, :]
 
     def look_up(table, at, index):
         row = jnp.broadcast_to(table[at : at + 1, :], (SLOTS_TILE, LANES))
         return jnp.take_along_axis(row, index, axis=1, mode="promise_in_bounds")
+
+    def merge(first, second, bit):
+        if first is None and second is None:
+            return None
+        zero = jnp.zeros((SLOTS_TILE, LANES), jnp.float32)
+        first = zero if first is None else first
+        second = zero if second is None else second
+        mask = (iota((SLOTS_TILE, LANES), 0) & bit) == 0
+        return jnp.where(mask, first, second) + pltpu.roll(jnp.where(mask, second, first), bit, 0)
 
     first, last = field(0), field(1)
     first_node, last_node = first.astype(jnp.int32), last.astype(jnp.int32)
@@ -353,58 +371,67 @@
         inverse = 1.0 / spread
         scale = size * spread
         hurdle = strike * inverse
-        rows = range(date * SLOTS_TILE, (date + 1) * SLOTS_TILE)
+        rows = [date * SLOTS + slot for slot in slots]
         starts = [(look_up(discount, at, first_node), look_up(running, at, first_node)) for at in rows]
         ends = [(look_up(discount, at, last_node), look_up(running, at, last_node)) for at in rows]
-        values = []
-        for (curve_start, sum_start), (curve_end, sum_end) in zip(starts, ends):
+        values = [None] * SLOTS
+        for slot, (curve_start, sum_start), (curve_end, sum_end) in zip(slots, starts, ends):
             float_leg, annuity = curve_start - curve_end, sum_end - sum_start
             standard = float_leg * pl.reciprocal(annuity) * inverse - hurdle
             size_of = jnp.abs(standard)
             power = jnp.full_like(size_of, TAIL[-1])
             for term in TAIL[-2::-1]:
                 power = power * size_of + term
-            values.append(scale * annuity * (0.5 * size_of + tilt * standard + jnp.exp2(power)))
-        for bit, mask in zip((1, 2, 4), masks):
-            values = [
-                jnp.where(mask, a, b) + pltpu.roll(jnp.where(mask, b, a), bit, 0)
-                for a, b in zip(values[::2], values[1::2])
-            ]
+            values[slot] = scale * annuity * (0.5 * size_of + tilt * standard + jnp.exp2(power))
+        for bit in (1, 2, 4):
+            values = [merge(a, b, bit) for a, b in zip(values[::2], values[1::2])]
         totals.append(values[0])
     return jnp.concatenate(totals, axis=0)
 
 
-def price(*refs):
-    refs, (grid, out, discount, running) = refs[:-4], refs[-4:]
+def set_tables(refs, grid, discount, running):
+    line = FIELDS * SLOTS_TILE + 1 + lax.axis_index("path")
+    lines = jnp.concatenate(
+        [ref[pl.ds(line, 1), :] for ref in refs] + [jnp.zeros((1, LANES), jnp.float32)] * (SLOTS - len(refs)), axis=0
+    )
+    shocks = [jnp.broadcast_to(lines[:, at : at + 1], (SLOTS, LANES)) for at in range(2 * DATES)]
+    shocks = jnp.stack([jnp.stack(shocks[:DATES]), jnp.stack(shocks[DATES:])])
+    discount[...], running[...] = tables(shocks, grid)
+
+
+def net(refs, totals):
     extra = FIELDS * SLOTS_TILE
-    me, core = lax.axis_index("trade"), lax.axis_index("path")
-    row = iota((SLOTS_TILE, LANES), 0)
-    lines = jnp.zeros((SLOTS_TILE, LANES), jnp.float32)
-    for ref, offset in zip(refs, [0] + offsets(core) + offsets(1 - core)[1:]):
-        line = jnp.broadcast_to(ref[pl.ds(extra + 1 + core, 1), :], (SLOTS_TILE, LANES))
-        lines = jnp.where(row == (me ^ offset), line, lines)
-    shocks = jnp.stack(
-        [
-            jnp.stack(
-                [
-                    jnp.broadcast_to(lines[:, at : at + 1], (SLOTS_TILE, LANES))
-                    for at in range(factor * DATES, (factor + 1) * DATES)
-                ]
-            )
-            for factor in range(2)
-        ]
-    )
-    discount[...], running[...] = tables(shocks, grid)
-    masks = [(row & bit) == 0 for bit in (1, 2, 4)]
     set_index = iota((SET_DEV, LANES), 0).astype(jnp.float32)
     one_hot = jnp.concatenate(
         [(set_index == ref[extra : extra + 1, :]).astype(jnp.bfloat16) for ref in refs], axis=1
     )
-    totals = jnp.concatenate([price_source(ref, discount, running, masks) for ref in refs], axis=1)
     netted = lax.dot_general(
-        split(totals, 3), one_hot, (((1,), (1,)), ((), ())), preferred_element_type=jnp.float32
-    )
-    out[...] = jnp.maximum(add_parts(netted, 3), 0.0)
+        split(jnp.concatenate(totals, axis=1), 3),
+        one_hot,
+        (((1,), (1,)), ((), ())),
+        preferred_element_type=jnp.float32,
+    )
+    return add_parts(netted, 3)
+
+
+def price_early(*refs):
+    refs, (grid, out, discount, running) = refs[:-4], refs[-4:]
+    set_tables(refs, grid, discount, running)
+    out[...] = net(refs, [price_source(ref, discount, running, range(EARLY)) for ref in refs])
+
+
+def price_late(*refs):
+    refs, (grid, early, out, discount, running) = refs[:-5], refs[-5:]
+    set_tables(refs, grid, discount, running)
+    totals = [
+        price_source(ref, discount, running, range(EARLY if at < EARLY else 0, SLOTS)) for at, ref in enumerate(refs)
+    ]
+    netted = jnp.maximum(net(refs, totals) + early[...], 0.0)
+    me = lax.axis_index("trade")
+    for slot, offset in enumerate(slot_offsets(lax.axis_index("path"))):
+        for date in range(DATES):
+            at = date * SLOTS + slot
+            out[pl.ds(date * SLOTS + (me ^ offset), 1), :] = netted[at : at + 1, :]
 
 
 def shards_by_trade(
@@ -426,10 +453,11 @@
         own_shocks,
     )
     message = jax.ShapeDtypeStruct((ROWS, LANES), jnp.float32)
+    near_message = jax.ShapeDtypeStruct((ROWS + SLOTS_TILE, LANES), jnp.float32)
     limit = pltpu.CompilerParams(vmem_limit_bytes=VMEM_BYTES)
     own, near, *far, grid = pl.pallas_call(
         pack,
-        out_shape=[message] * (2 + len(FAR)) + [jax.ShapeDtypeStruct((3, SLOTS_TILE, GRID), jnp.float32)],
+        out_shape=[message, near_message] + [message] * len(FAR) + [jax.ShapeDtypeStruct((3, SLOTS_TILE, GRID), jnp.float32)],
         in_specs=[pl.BlockSpec(memory_space=pltpu.HBM)] * len(fields),
         scratch_shapes=[pltpu.VMEM(field.shape, field.dtype) for field in fields]
         + [pltpu.SemaphoreType.DMA((len(fields),))],
@@ -450,16 +478,23 @@
         turns = [(2 * at + core, 2 * (at ^ pair[core]) + core) for at in range(owners) for core in range(2)]
         far_in.append(lax.ppermute(piece, ("trade", "path"), turns))
     handed = [lax.ppermute(piece, "path", swap) for piece in far_in]
+    result = jax.ShapeDtypeStruct((dates_count * SLOTS, SET_DEV), jnp.float32)
+    table = pltpu.VMEM((dates_count * SLOTS, GRID), jnp.float32)
+    slots = (own, *far_in, *handed[:-1], near_in, handed[-1])
+    early = pl.pallas_call(
+        price_early,
+        out_shape=result,
+        scratch_shapes=[table] * 2,
+        compiler_params=limit,
+        name="price_early",
+    )(*slots[:EARLY], grid)
     netted = pl.pallas_call(
-        price,
-        out_shape=jax.ShapeDtypeStruct((dates_count * SLOTS_TILE, SET_DEV), jnp.float32),
-        scratch_shapes=[
-            pltpu.VMEM((dates_count * SLOTS_TILE, GRID), jnp.float32),
-            pltpu.VMEM((dates_count * SLOTS_TILE, GRID), jnp.float32),
-        ],
+        price_late,
+        out_shape=result,
+        scratch_shapes=[table] * 2,
         compiler_params=limit,
-        name="price",
-    )(own, near_in, *far_in, *handed, grid)
+        name="price_late",
+    )(*slots, grid, early)
     return netted.reshape(dates_count, SLOTS_TILE, SET_DEV).transpose(2, 0, 1)
 
 

time: 14.8 us -> 14.4 us (0.973)
  waiting for transfers between devices: 1.98 us -> 1.15 us
  Pallas kernels: 2.9 us -> 3.4 us
    ppermute x1, waiting for transfers between devices: 0.68 us -> 0.01 us  [shards_by_trade(): lax.ppermute(near, 'trade', [(at, at ^ NEAR) for at in range(owners)])]
    pallas_call x2 -> x3, Pallas kernels: 2.82 us -> 3.32 us  [the longest x1 1.4 us: shards_by_trade(): pl.pallas_call(price_late, out_shape=result, scratch_shapes=[table] * 2,...]
    ppermute x3, waiting for transfers between devices: 0.18 us -> 0.02 us  [shards_by_trade(): handed = [lax.ppermute(piece, 'path', swap) for piece in far_in]]
  transfers between devices with their start and end apart: 8 -> 8, of which waited for: 3 -> 1; matrix products, arithmetic and copies ran while one was open for 0% -> 0% of each run, Pallas kernels for 7% -> 14%
where the time goes in v5:
time: 14.4 us; the launch traced here: 14.2 us
  starting transfers between devices  9.67 us (67%)
  Pallas kernels  3.4 us (24%)
  waiting for transfers between devices  1.15 us (8%)
    ppermute x3, starting transfers between devices, shards_by_trade(): far_in.append(lax.ppermute(piece, ('trade', 'path'), turns))  6.75 us
    ppermute x1, starting transfers between devices, shards_by_trade(): lax.ppermute(near, 'trade', [(at, at ^ NEAR) for at in range(owners)])  1.49 us
    pallas_call x1, Pallas kernels, shards_by_trade(): pl.pallas_call(price_late, out_shape=result, scratch_shapes=[table] * 2,...  1.4 us
    ppermute x3, waiting for transfers between devices, shards_by_trade(): far_in.append(lax.ppermute(piece, ('trade', 'path'), turns))  1.13 us
    pallas_call x1, Pallas kernels, shards_by_trade(): pl.pallas_call(pack, out_shape=[message, near_message] + [message] * len(...  1.09 us
    ppermute x3, starting transfers between devices, shards_by_trade(): handed = [lax.ppermute(piece, 'path', swap) for piece in far_in]  0.98 us
    pallas_call x1, Pallas kernels, shards_by_trade(): pl.pallas_call(price_early, out_shape=result, scratch_shapes=[table] * 2,...  0.83 us
    ppermute x1, starting transfers between devices, shards_by_trade(): other_shocks = lax.ppermute(shocks, 'path', swap).reshape(2, dates_count)  0.45 us
  transfers between devices with their start and end apart: 8, of which 1 were waited for; matrix products, arithmetic and copies ran while one was open for 0% of the time, Pallas kernels for 14%

profile of v5, /device:TPU:0, one launch (start us, length us, event | category | flops | bytes accessed | tf_op | source)
XLA Modules:
  0.0 14.2 jit_solution(18102902990259976255)
XLA Ops:
  0.0 0.5 %collective-permute-start = (f32[2,2,1,1]{1,3,2,0:T(1,128)}, f32[2,2,1,1]{1,3,2,0:T(1,128)S(1)}, u32[]{:S(2)}, u32[]{:S(2)}) collective-permute-start(f32[2,2,1,1]{1,3,2,0:T(1,128)} %param.9), channel_id=1, source_target_pairs={{0,1},{1,0},{2,3},{3,2},{4,5},{5,4},{6,7},{7,6},{8,9},{9,8},{10,11... | collective-permute-start | bytes 56 | tf_op jit(solution)/shard_map/ppermute | solution.py:443
  0.5 1.1 %pack.1 = (f32[56,128]{1,0:T(8,128)S(1)}, f32[64,128]{1,0:T(8,128)S(1)}, f32[56,128]{1,0:T(8,128)S(1)}, f32[56,128]{1,0:T(8,128)S(1)}, f32[56,128]{1,0:T(8,128)S(1)}, /*index=5*/f32[3,8,128]{2,1,0:T(8,128)S(1)}) custom-call(s32[16,512]{1,0:T(8,128)} %bitcast.14, s32[16,512]{1,0:T(8,128)} %bitcast.15, s32[16,512]{1,0:T(8,128)} %bitcast.16, ...), custom_call_target="tpu_custom_call" | custom-call | tf_op jit(solution)/shard_map/pack/pallas_call | solution.py:458
  1.6 0.0 collective-permute-done
  1.6 0.1 add_shocks.1
  1.6 2.8 %collective-permute-start.1 = (f32[56,128]{1,0:T(8,128)S(1)}, f32[56,128]{1,0:T(8,128)S(1)}, u32[]{:S(2)}, u32[]{:S(2)}) collective-permute-start(f32[56,128]{1,0:T(8,128)S(1)} %get-tuple-element.18), channel_id=1, source_target_pairs={{0,4},{1,9},{2,6},{3,11},{4,0},{5,13},{6,2},{7,15},{8,12},{9,1},{1... | collective-permute-start | bytes 86024 | tf_op jit(solution)/shard_map/ppermute | solution.py:479
  4.5 1.4 %collective-permute-start.2 = (f32[56,128]{1,0:T(8,128)S(1)}, f32[56,128]{1,0:T(8,128)S(1)}, u32[]{:S(2)}, u32[]{:S(2)}) collective-permute-start(f32[56,128]{1,0:T(8,128)S(1)} %get-tuple-element.19), channel_id=1, source_target_pairs={{0,6},{1,13},{2,4},{3,15},{4,2},{5,9},{6,0},{7,11},{8,14},{9,5},{1... | collective-permute-start | bytes 86024 | tf_op jit(solution)/shard_map/ppermute | solution.py:479
  5.8 2.6 %collective-permute-start.3 = (f32[56,128]{1,0:T(8,128)S(1)}, f32[56,128]{1,0:T(8,128)S(1)}, u32[]{:S(2)}, u32[]{:S(2)}) collective-permute-start(f32[56,128]{1,0:T(8,128)S(1)} %get-tuple-element.20), channel_id=1, source_target_pairs={{0,10},{1,15},{2,8},{3,13},{4,14},{5,11},{6,12},{7,9},{8,2},{9,7},... | collective-permute-start | bytes 86024 | tf_op jit(solution)/shard_map/ppermute | solution.py:479
  8.4 1.5 %collective-permute-start.6 = (f32[64,128]{1,0:T(8,128)S(1)}, f32[64,128]{1,0:T(8,128)S(1)}, u32[]{:S(2)}, u32[]{:S(2)}) collective-permute-start(f32[64,128]{1,0:T(8,128)S(1)} %get-tuple-element.21), channel_id=1, source_target_pairs={{0,2},{2,0},{4,6},{6,4},{8,10},{10,8},{12,14},{14,12},{1,3},{3,1},... | collective-permute-start | bytes 98312 | tf_op jit(solution)/shard_map/ppermute | solution.py:468
  9.9 0.0 collective-permute-done.1.refs_1_
  9.9 0.0 collective-permute-start.4
  9.9 0.0 collective-permute-done.2.refs_2_
  9.9 0.5 %collective-permute-start.5 = (f32[56,128]{1,0:T(8,128)S(1)}, f32[56,128]{1,0:T(8,128)S(1)}, u32[]{:S(2)}, u32[]{:S(2)}) collective-permute-start(f32[56,128]{1,0:T(8,128)S(1)} %collective-permute-done.2.refs_2_), channel_id=1, source_target_pairs={{0,1},{1,0},{2,3},{3,2},{4,5},{5,4},{6,7},{7,6},{8,9},{9,8},{10,11... | collective-permute-start | bytes 86024 | tf_op jit(solution)/shard_map/ppermute | solution.py:480
  10.4 1.1 %collective-permute-done.3.refs_3_ = f32[56,128]{1,0:T(8,128)S(1)} collective-permute-done((f32[56,128]{1,0:T(8,128)S(1)}, f32[56,128]{1,0:T(8,128)S(1)}, u32[]{:S(2)}, u32[]{:S(2)}) %collective-permute-start.3) | collective-permute-done | bytes 28704 | tf_op jit(solution)/shard_map/ppermute | solution.py:479
  11.5 0.5 %collective-permute-start.7 = (f32[56,128]{1,0:T(8,128)S(1)}, f32[56,128]{1,0:T(8,128)S(1)}, u32[]{:S(2)}, u32[]{:S(2)}) collective-permute-start(f32[56,128]{1,0:T(8,128)S(1)} %collective-permute-done.3.refs_3_), channel_id=1, source_target_pairs={{0,1},{1,0},{2,3},{3,2},{4,5},{5,4},{6,7},{7,6},{8,9},{9,8},{10,11... | collective-permute-start | bytes 86024 | tf_op jit(solution)/shard_map/ppermute | solution.py:480
  12.0 0.0 collective-permute-done.4.refs_4_
  12.0 0.0 collective-permute-done.5.refs_5_
  12.0 0.8 %price_early.1.refs_9_ = f32[16,32]{1,0:T(8,128)S(1)} custom-call(f32[56,128]{1,0:T(8,128)S(1)} %get-tuple-element.14.refs_0_, f32[56,128]{1,0:T(8,128)S(1)} %collective-permute-done.1.refs_1_, f32[56,128]{1,0:T(8,128)S(1)} %collective-permute-done.2.refs_2_, f32[56,128]{1,0:T(8,128)S(1)} %collective-permute-done.3.refs_3_, ...), custom_call_target="tpu_custom_call" | custom-call | tf_op jit(solution)/shard_map/price_early/pallas_call | solution.py:484
  12.8 0.0 collective-permute-done.6.refs_6_
  12.8 0.0 collective-permute-done.7.refs_7_
  12.8 1.4 %price_late.1 = f32[16,32]{1,0:T(8,128)} custom-call(f32[56,128]{1,0:T(8,128)S(1)} %get-tuple-element.14.refs_0_, f32[56,128]{1,0:T(8,128)S(1)} %collective-permute-done.1.refs_1_, f32[56,128]{1,0:T(8,128)S(1)} %collective-permute-done.2.refs_2_, f32[56,128]{1,0:T(8,128)S(1)} %collective-permute-done.3.refs_3_, ...), custom_call_target="tpu_custom_call" | custom-call | tf_op jit(solution)/shard_map/price_late/pallas_call | solution.py:491
Async XLA Ops:
  0.0 1.6 %collective-permute-start = (f32[2,2,1,1]{1,3,2,0:T(1,128)}, f32[2,2,1,1]{1,3,2,0:T(1,128)S(1)}, u32[]{:S(2)}, u32[]{:S(2)}) collective-permute-start(f32[2,2,1,1]{1,3,2,0:T(1,128)} %param.9), channel_id=1, source_target_pairs={{0,1},{1,0},{2,3},{3,2},{4,5},{5,4},{6,7},{7,6},{8,9},{9,8},{10,11... | collective-permute-start | bytes 56 | tf_op jit(solution)/shard_map/ppermute | solution.py:443
  1.6 8.2 %collective-permute-start.1 = (f32[56,128]{1,0:T(8,128)S(1)}, f32[56,128]{1,0:T(8,128)S(1)}, u32[]{:S(2)}, u32[]{:S(2)}) collective-permute-start(f32[56,128]{1,0:T(8,128)S(1)} %get-tuple-element.18), channel_id=1, source_target_pairs={{0,4},{1,9},{2,6},{3,11},{4,0},{5,13},{6,2},{7,15},{8,12},{9,1},{1... | collective-permute-start | bytes 86024 | tf_op jit(solution)/shard_map/ppermute | solution.py:479
  4.5 5.5 %collective-permute-start.2 = (f32[56,128]{1,0:T(8,128)S(1)}, f32[56,128]{1,0:T(8,128)S(1)}, u32[]{:S(2)}, u32[]{:S(2)}) collective-permute-start(f32[56,128]{1,0:T(8,128)S(1)} %get-tuple-element.19), channel_id=1, source_target_pairs={{0,6},{1,13},{2,4},{3,15},{4,2},{5,9},{6,0},{7,11},{8,14},{9,5},{1... | collective-permute-start | bytes 86024 | tf_op jit(solution)/shard_map/ppermute | solution.py:479
  5.8 5.7 %collective-permute-start.3 = (f32[56,128]{1,0:T(8,128)S(1)}, f32[56,128]{1,0:T(8,128)S(1)}, u32[]{:S(2)}, u32[]{:S(2)}) collective-permute-start(f32[56,128]{1,0:T(8,128)S(1)} %get-tuple-element.20), channel_id=1, source_target_pairs={{0,10},{1,15},{2,8},{3,13},{4,14},{5,11},{6,12},{7,9},{8,2},{9,7},... | collective-permute-start | bytes 86024 | tf_op jit(solution)/shard_map/ppermute | solution.py:479
  8.4 4.4 %collective-permute-start.6 = (f32[64,128]{1,0:T(8,128)S(1)}, f32[64,128]{1,0:T(8,128)S(1)}, u32[]{:S(2)}, u32[]{:S(2)}) collective-permute-start(f32[64,128]{1,0:T(8,128)S(1)} %get-tuple-element.21), channel_id=1, source_target_pairs={{0,2},{2,0},{4,6},{6,4},{8,10},{10,8},{12,14},{14,12},{1,3},{3,1},... | collective-permute-start | bytes 98312 | tf_op jit(solution)/shard_map/ppermute | solution.py:468
  9.9 2.1 %collective-permute-start.4 = (f32[56,128]{1,0:T(8,128)S(1)}, f32[56,128]{1,0:T(8,128)S(1)}, u32[]{:S(2)}, u32[]{:S(2)}) collective-permute-start(f32[56,128]{1,0:T(8,128)S(1)} %collective-permute-done.1.refs_1_), channel_id=1, source_target_pairs={{0,1},{1,0},{2,3},{3,2},{4,5},{5,4},{6,7},{7,6},{8,9},{9,8},{10,11... | collective-permute-start | bytes 86024 | tf_op jit(solution)/shard_map/ppermute | solution.py:480
  9.9 2.1 %collective-permute-start.5 = (f32[56,128]{1,0:T(8,128)S(1)}, f32[56,128]{1,0:T(8,128)S(1)}, u32[]{:S(2)}, u32[]{:S(2)}) collective-permute-start(f32[56,128]{1,0:T(8,128)S(1)} %collective-permute-done.2.refs_2_), channel_id=1, source_target_pairs={{0,1},{1,0},{2,3},{3,2},{4,5},{5,4},{6,7},{7,6},{8,9},{9,8},{10,11... | collective-permute-start | bytes 86024 | tf_op jit(solution)/shard_map/ppermute | solution.py:480
  11.5 1.3 %collective-permute-start.7 = (f32[56,128]{1,0:T(8,128)S(1)}, f32[56,128]{1,0:T(8,128)S(1)}, u32[]{:S(2)}, u32[]{:S(2)}) collective-permute-start(f32[56,128]{1,0:T(8,128)S(1)} %collective-permute-done.3.refs_3_), channel_id=1, source_target_pairs={{0,1},{1,0},{2,3},{3,2},{4,5},{5,4},{6,7},{7,6},{8,9},{9,8},{10,11... | collective-permute-start | bytes 86024 | tf_op jit(solution)/shard_map/ppermute | solution.py:480

commit v6 on v5

--- a/solution.py
+++ b/solution.py
@@ -259,19 +259,18 @@
     for out, offset in zip(outs, [0] + offsets(core)):
         owner = me ^ offset
         cut = pl.ds(pl.multiple_of(owner // 2 * LANES, LANES), LANES)
-        odd = owner % 2
-
-        def both(low_half, high_half):
-            return jnp.where(
-                low, pltpu.roll(low_half, half * odd, 1), pltpu.roll(high_half, half * (1 - odd), 1)
-            )
+
+        here = low == (owner % 2 == 0)
+
+        def both(in_place, turned):
+            return jnp.where(here, in_place, pltpu.roll(turned, half, 1))
 
         def field(ref):
             return both(ref[:SLOTS_TILE, cut], ref[SLOTS_TILE:, cut])
 
         lives = jnp.broadcast_to(live[:, cut], (SLOTS_TILE, LANES))
         sets = jnp.broadcast_to(group[:, cut], (SLOTS_TILE, LANES))
-        slot = row + jnp.where(low, 0, SLOTS_TILE)
+        slot = row + jnp.where(here, 0, SLOTS_TILE)
         first, kinds = field(start), field(kind)
         size = jnp.where(kinds == 2, 2.0, 1.0) * field(notional)
         tiles = (
@@ -344,7 +343,7 @@
     return both, add_parts(sums, 3)
 
 
-def price_source(ref, discount, running, slots):
+def price_source(ref, tables_of, slots):
     def field(at):
         return ref[at * SLOTS_TILE : (at + 1) * SLOTS_TILE, :]
 
@@ -371,9 +370,9 @@
         inverse = 1.0 / spread
         scale = size * spread
         hurdle = strike * inverse
-        rows = [date * SLOTS + slot for slot in slots]
-        starts = [(look_up(discount, at, first_node), look_up(running, at, first_node)) for at in rows]
-        ends = [(look_up(discount, at, last_node), look_up(running, at, last_node)) for at in rows]
+        rows = [(*tables_of(slot), date * SLOTS + slot) for slot in slots]
+        starts = [(look_up(curve, at, first_node), look_up(sums, at, first_node)) for curve, sums, at in rows]
+        ends = [(look_up(curve, at, last_node), look_up(sums, at, last_node)) for curve, sums, at in rows]
         values = [None] * SLOTS
         for slot, (curve_start, sum_start), (curve_end, sum_end) in zip(slots, starts, ends):
             float_leg, annuity = curve_start - curve_end, sum_end - sum_start
@@ -391,9 +390,8 @@
 
 def set_tables(refs, grid, discount, running):
     line = FIELDS * SLOTS_TILE + 1 + lax.axis_index("path")
-    lines = jnp.concatenate(
-        [ref[pl.ds(line, 1), :] for ref in refs] + [jnp.zeros((1, LANES), jnp.float32)] * (SLOTS - len(refs)), axis=0
-    )
+    empty = jnp.zeros((1, LANES), jnp.float32)
+    lines = jnp.concatenate([empty if ref is None else ref[pl.ds(line, 1), :] for ref in refs], axis=0)
     shocks = [jnp.broadcast_to(lines[:, at : at + 1], (SLOTS, LANES)) for at in range(2 * DATES)]
     shocks = jnp.stack([jnp.stack(shocks[:DATES]), jnp.stack(shocks[DATES:])])
     discount[...], running[...] = tables(shocks, grid)
@@ -416,16 +414,19 @@
 
 def price_early(*refs):
     refs, (grid, out, discount, running) = refs[:-4], refs[-4:]
-    set_tables(refs, grid, discount, running)
-    out[...] = net(refs, [price_source(ref, discount, running, range(EARLY)) for ref in refs])
+    set_tables([*refs, *[None] * (SLOTS - EARLY)], grid, discount, running)
+    out[...] = net(refs, [price_source(ref, lambda slot: (discount, running), range(EARLY)) for ref in refs])
 
 
 def price_late(*refs):
-    refs, (grid, early, out, discount, running) = refs[:-5], refs[-5:]
-    set_tables(refs, grid, discount, running)
-    totals = [
-        price_source(ref, discount, running, range(EARLY if at < EARLY else 0, SLOTS)) for at, ref in enumerate(refs)
-    ]
+    refs, (grid, early, discount, running, out, late_discount, late_running) = refs[:-7], refs[-7:]
+    set_tables([*[None] * EARLY, *refs[EARLY:]], grid, late_discount, late_running)
+
+    def tables_of(slot):
+        return (discount, running) if slot < EARLY else (late_discount, late_running)
+
+    totals = [price_source(ref, tables_of, range(SLOTS)) for ref in refs[EARLY:]]
+    totals = [price_source(ref, tables_of, range(EARLY, SLOTS)) for ref in refs[:EARLY]] + totals
     netted = jnp.maximum(net(refs, totals) + early[...], 0.0)
     me = lax.axis_index("trade")
     for slot, offset in enumerate(slot_offsets(lax.axis_index("path"))):
@@ -479,22 +480,21 @@
         far_in.append(lax.ppermute(piece, ("trade", "path"), turns))
     handed = [lax.ppermute(piece, "path", swap) for piece in far_in]
     result = jax.ShapeDtypeStruct((dates_count * SLOTS, SET_DEV), jnp.float32)
-    table = pltpu.VMEM((dates_count * SLOTS, GRID), jnp.float32)
+    table = jax.ShapeDtypeStruct((dates_count * SLOTS, GRID), jnp.float32)
     slots = (own, *far_in, *handed[:-1], near_in, handed[-1])
     early = pl.pallas_call(
         price_early,
-        out_shape=result,
-        scratch_shapes=[table] * 2,
+        out_shape=[result, table, table],
         compiler_params=limit,
         name="price_early",
     )(*slots[:EARLY], grid)
     netted = pl.pallas_call(
         price_late,
         out_shape=result,
-        scratch_shapes=[table] * 2,
+        scratch_shapes=[pltpu.VMEM(table.shape, table.dtype)] * 2,
         compiler_params=limit,
         name="price_late",
-    )(*slots, grid, early)
+    )(*slots, grid, *early)
     return netted.reshape(dates_count, SLOTS_TILE, SET_DEV).transpose(2, 0, 1)
 
 

time: 14.4 us -> 14.3 us (level)
  transfers between devices with their start and end apart: 8 -> 8, of which waited for: 1 -> 1; matrix products, arithmetic and copies ran while one was open for 0% -> 0% of each run, Pallas kernels for 14% -> 13%
where the time goes in v6:
time: 14.3 us; the launch traced here: 14.1 us
  starting transfers between devices  9.69 us (68%)
  Pallas kernels  3.27 us (23%)
  waiting for transfers between devices  1.13 us (8%)
    ppermute x3, starting transfers between devices, shards_by_trade(): far_in.append(lax.ppermute(piece, ('trade', 'path'), turns))  6.78 us
    ppermute x1, starting transfers between devices, shards_by_trade(): lax.ppermute(near, 'trade', [(at, at ^ NEAR) for at in range(owners)])  1.49 us
    pallas_call x1, Pallas kernels, shards_by_trade(): pl.pallas_call(price_late, out_shape=result, scratch_shapes=[pltpu.VMEM(t...  1.3 us
    ppermute x3, waiting for transfers between devices, shards_by_trade(): far_in.append(lax.ppermute(piece, ('trade', 'path'), turns))  1.1 us
    pallas_call x1, Pallas kernels, shards_by_trade(): pl.pallas_call(pack, out_shape=[message, near_message] + [message] * len(...  1.06 us
    ppermute x3, starting transfers between devices, shards_by_trade(): handed = [lax.ppermute(piece, 'path', swap) for piece in far_in]  0.97 us
    pallas_call x1, Pallas kernels, shards_by_trade(): pl.pallas_call(price_early, out_shape=[result, table, table], compiler_pa...  0.83 us
    ppermute x1, starting transfers between devices, shards_by_trade(): other_shocks = lax.ppermute(shocks, 'path', swap).reshape(2, dates_count)  0.45 us
  transfers between devices with their start and end apart: 8, of which 1 were waited for; matrix products, arithmetic and copies ran while one was open for 0% of the time, Pallas kernels for 13%

profile of v6, /device:TPU:0, one launch (start us, length us, event | category | flops | bytes accessed | tf_op | source)
XLA Modules:
  0.0 14.1 jit_solution(10847750233661164975)
XLA Ops:
  0.0 0.5 %collective-permute-start = (f32[2,2,1,1]{1,3,2,0:T(1,128)}, f32[2,2,1,1]{1,3,2,0:T(1,128)S(1)}, u32[]{:S(2)}, u32[]{:S(2)}) collective-permute-start(f32[2,2,1,1]{1,3,2,0:T(1,128)} %param.9), channel_id=1, source_target_pairs={{0,1},{1,0},{2,3},{3,2},{4,5},{5,4},{6,7},{7,6},{8,9},{9,8},{10,11... | collective-permute-start | bytes 56 | tf_op jit(solution)/shard_map/ppermute | solution.py:444
  0.5 1.1 %pack.1 = (f32[56,128]{1,0:T(8,128)S(1)}, f32[64,128]{1,0:T(8,128)S(1)}, f32[56,128]{1,0:T(8,128)S(1)}, f32[56,128]{1,0:T(8,128)S(1)}, f32[56,128]{1,0:T(8,128)S(1)}, /*index=5*/f32[3,8,128]{2,1,0:T(8,128)S(1)}) custom-call(s32[16,512]{1,0:T(8,128)} %bitcast.14, s32[16,512]{1,0:T(8,128)} %bitcast.15, s32[16,512]{1,0:T(8,128)} %bitcast.16, ...), custom_call_target="tpu_custom_call" | custom-call | tf_op jit(solution)/shard_map/pack/pallas_call | solution.py:459
  1.5 0.0 collective-permute-done
  1.5 0.1 add_shocks.1
  1.6 2.8 %collective-permute-start.1 = (f32[56,128]{1,0:T(8,128)S(1)}, f32[56,128]{1,0:T(8,128)S(1)}, u32[]{:S(2)}, u32[]{:S(2)}) collective-permute-start(f32[56,128]{1,0:T(8,128)S(1)} %get-tuple-element.21), channel_id=1, source_target_pairs={{0,4},{1,9},{2,6},{3,11},{4,0},{5,13},{6,2},{7,15},{8,12},{9,1},{1... | collective-permute-start | bytes 86024 | tf_op jit(solution)/shard_map/ppermute | solution.py:480
  4.5 1.4 %collective-permute-start.2 = (f32[56,128]{1,0:T(8,128)S(1)}, f32[56,128]{1,0:T(8,128)S(1)}, u32[]{:S(2)}, u32[]{:S(2)}) collective-permute-start(f32[56,128]{1,0:T(8,128)S(1)} %get-tuple-element.22), channel_id=1, source_target_pairs={{0,6},{1,13},{2,4},{3,15},{4,2},{5,9},{6,0},{7,11},{8,14},{9,5},{1... | collective-permute-start | bytes 86024 | tf_op jit(solution)/shard_map/ppermute | solution.py:480
  5.8 2.6 %collective-permute-start.3 = (f32[56,128]{1,0:T(8,128)S(1)}, f32[56,128]{1,0:T(8,128)S(1)}, u32[]{:S(2)}, u32[]{:S(2)}) collective-permute-start(f32[56,128]{1,0:T(8,128)S(1)} %get-tuple-element.23), channel_id=1, source_target_pairs={{0,10},{1,15},{2,8},{3,13},{4,14},{5,11},{6,12},{7,9},{8,2},{9,7},... | collective-permute-start | bytes 86024 | tf_op jit(solution)/shard_map/ppermute | solution.py:480
  8.4 1.5 %collective-permute-start.6 = (f32[64,128]{1,0:T(8,128)S(1)}, f32[64,128]{1,0:T(8,128)S(1)}, u32[]{:S(2)}, u32[]{:S(2)}) collective-permute-start(f32[64,128]{1,0:T(8,128)S(1)} %get-tuple-element.24), channel_id=1, source_target_pairs={{0,2},{2,0},{4,6},{6,4},{8,10},{10,8},{12,14},{14,12},{1,3},{3,1},... | collective-permute-start | bytes 98312 | tf_op jit(solution)/shard_map/ppermute | solution.py:469
  9.9 0.0 collective-permute-done.1.refs_1_
  9.9 0.0 collective-permute-start.4
  9.9 0.0 collective-permute-done.2.refs_2_
  9.9 0.5 %collective-permute-start.5 = (f32[56,128]{1,0:T(8,128)S(1)}, f32[56,128]{1,0:T(8,128)S(1)}, u32[]{:S(2)}, u32[]{:S(2)}) collective-permute-start(f32[56,128]{1,0:T(8,128)S(1)} %collective-permute-done.2.refs_2_), channel_id=1, source_target_pairs={{0,1},{1,0},{2,3},{3,2},{4,5},{5,4},{6,7},{7,6},{8,9},{9,8},{10,11... | collective-permute-start | bytes 86024 | tf_op jit(solution)/shard_map/ppermute | solution.py:481
  10.4 1.1 %collective-permute-done.3.refs_3_ = f32[56,128]{1,0:T(8,128)S(1)} collective-permute-done((f32[56,128]{1,0:T(8,128)S(1)}, f32[56,128]{1,0:T(8,128)S(1)}, u32[]{:S(2)}, u32[]{:S(2)}) %collective-permute-start.3) | collective-permute-done | bytes 28704 | tf_op jit(solution)/shard_map/ppermute | solution.py:480
  11.5 0.5 %collective-permute-start.7 = (f32[56,128]{1,0:T(8,128)S(1)}, f32[56,128]{1,0:T(8,128)S(1)}, u32[]{:S(2)}, u32[]{:S(2)}) collective-permute-start(f32[56,128]{1,0:T(8,128)S(1)} %collective-permute-done.3.refs_3_), channel_id=1, source_target_pairs={{0,1},{1,0},{2,3},{3,2},{4,5},{5,4},{6,7},{7,6},{8,9},{9,8},{10,11... | collective-permute-start | bytes 86024 | tf_op jit(solution)/shard_map/ppermute | solution.py:481
  12.0 0.0 collective-permute-done.4.refs_4_
  12.0 0.0 collective-permute-done.5.refs_5_
  12.0 0.8 %price_early.1 = (f32[16,32]{1,0:T(8,128)S(1)}, f32[16,128]{1,0:T(8,128)S(1)}, f32[16,128]{1,0:T(8,128)S(1)}) custom-call(f32[56,128]{1,0:T(8,128)S(1)} %get-tuple-element.17.refs_0_, f32[56,128]{1,0:T(8,128)S(1)} %collective-permute-done.1.refs_1_, f32[56,128]{1,0:T(8,128)S(1)} %collective-permute-done.2.refs_2_, ...), custom_call_target="tpu_custom_call" | custom-call | tf_op jit(solution)/shard_map/price_early/pallas_call | solution.py:485
  12.8 0.0 collective-permute-done.6.refs_6_
  12.8 0.0 collective-permute-done.7.refs_7_
  12.8 1.3 %price_late.1 = f32[16,32]{1,0:T(8,128)} custom-call(f32[56,128]{1,0:T(8,128)S(1)} %get-tuple-element.17.refs_0_, f32[56,128]{1,0:T(8,128)S(1)} %collective-permute-done.1.refs_1_, f32[56,128]{1,0:T(8,128)S(1)} %collective-permute-done.2.refs_2_, f32[56,128]{1,0:T(8,128)S(1)} %collective-permute-done.3.refs_3_, ...), custom_call_target="tpu_custom_call" | custom-call | tf_op jit(solution)/shard_map/price_late/pallas_call | solution.py:491
Async XLA Ops:
  0.0 1.5 %collective-permute-start = (f32[2,2,1,1]{1,3,2,0:T(1,128)}, f32[2,2,1,1]{1,3,2,0:T(1,128)S(1)}, u32[]{:S(2)}, u32[]{:S(2)}) collective-permute-start(f32[2,2,1,1]{1,3,2,0:T(1,128)} %param.9), channel_id=1, source_target_pairs={{0,1},{1,0},{2,3},{3,2},{4,5},{5,4},{6,7},{7,6},{8,9},{9,8},{10,11... | collective-permute-start | bytes 56 | tf_op jit(solution)/shard_map/ppermute | solution.py:444
  1.6 8.3 %collective-permute-start.1 = (f32[56,128]{1,0:T(8,128)S(1)}, f32[56,128]{1,0:T(8,128)S(1)}, u32[]{:S(2)}, u32[]{:S(2)}) collective-permute-start(f32[56,128]{1,0:T(8,128)S(1)} %get-tuple-element.21), channel_id=1, source_target_pairs={{0,4},{1,9},{2,6},{3,11},{4,0},{5,13},{6,2},{7,15},{8,12},{9,1},{1... | collective-permute-start | bytes 86024 | tf_op jit(solution)/shard_map/ppermute | solution.py:480
  4.5 5.4 %collective-permute-start.2 = (f32[56,128]{1,0:T(8,128)S(1)}, f32[56,128]{1,0:T(8,128)S(1)}, u32[]{:S(2)}, u32[]{:S(2)}) collective-permute-start(f32[56,128]{1,0:T(8,128)S(1)} %get-tuple-element.22), channel_id=1, source_target_pairs={{0,6},{1,13},{2,4},{3,15},{4,2},{5,9},{6,0},{7,11},{8,14},{9,5},{1... | collective-permute-start | bytes 86024 | tf_op jit(solution)/shard_map/ppermute | solution.py:480
  5.8 5.7 %collective-permute-start.3 = (f32[56,128]{1,0:T(8,128)S(1)}, f32[56,128]{1,0:T(8,128)S(1)}, u32[]{:S(2)}, u32[]{:S(2)}) collective-permute-start(f32[56,128]{1,0:T(8,128)S(1)} %get-tuple-element.23), channel_id=1, source_target_pairs={{0,10},{1,15},{2,8},{3,13},{4,14},{5,11},{6,12},{7,9},{8,2},{9,7},... | collective-permute-start | bytes 86024 | tf_op jit(solution)/shard_map/ppermute | solution.py:480
  8.4 4.4 %collective-permute-start.6 = (f32[64,128]{1,0:T(8,128)S(1)}, f32[64,128]{1,0:T(8,128)S(1)}, u32[]{:S(2)}, u32[]{:S(2)}) collective-permute-start(f32[64,128]{1,0:T(8,128)S(1)} %get-tuple-element.24), channel_id=1, source_target_pairs={{0,2},{2,0},{4,6},{6,4},{8,10},{10,8},{12,14},{14,12},{1,3},{3,1},... | collective-permute-start | bytes 98312 | tf_op jit(solution)/shard_map/ppermute | solution.py:469
  9.9 2.1 %collective-permute-start.4 = (f32[56,128]{1,0:T(8,128)S(1)}, f32[56,128]{1,0:T(8,128)S(1)}, u32[]{:S(2)}, u32[]{:S(2)}) collective-permute-start(f32[56,128]{1,0:T(8,128)S(1)} %collective-permute-done.1.refs_1_), channel_id=1, source_target_pairs={{0,1},{1,0},{2,3},{3,2},{4,5},{5,4},{6,7},{7,6},{8,9},{9,8},{10,11... | collective-permute-start | bytes 86024 | tf_op jit(solution)/shard_map/ppermute | solution.py:481
  9.9 2.1 %collective-permute-start.5 = (f32[56,128]{1,0:T(8,128)S(1)}, f32[56,128]{1,0:T(8,128)S(1)}, u32[]{:S(2)}, u32[]{:S(2)}) collective-permute-start(f32[56,128]{1,0:T(8,128)S(1)} %collective-permute-done.2.refs_2_), channel_id=1, source_target_pairs={{0,1},{1,0},{2,3},{3,2},{4,5},{5,4},{6,7},{7,6},{8,9},{9,8},{10,11... | collective-permute-start | bytes 86024 | tf_op jit(solution)/shard_map/ppermute | solution.py:481
  11.5 1.3 %collective-permute-start.7 = (f32[56,128]{1,0:T(8,128)S(1)}, f32[56,128]{1,0:T(8,128)S(1)}, u32[]{:S(2)}, u32[]{:S(2)}) collective-permute-start(f32[56,128]{1,0:T(8,128)S(1)} %collective-permute-done.3.refs_3_), channel_id=1, source_target_pairs={{0,1},{1,0},{2,3},{3,2},{4,5},{5,4},{6,7},{7,6},{8,9},{9,8},{10,11... | collective-permute-start | bytes 86024 | tf_op jit(solution)/shard_map/ppermute | solution.py:481

commit v7 on v6

--- a/solution.py
+++ b/solution.py
@@ -198,7 +198,7 @@
 ROWS = (FIELDS + 1) * SLOTS_TILE
 INPUTS = range(9)
 NEAR = 1
-FAR = ((2, 4), (3, 6), (5, 7))
+FAR = ((3, 4), (2, 6), (5, 7))
 SLOTS = 8
 EARLY = 6
 DATES = 2

time: 14.3 us -> 14.3 us (level)
  no operation moved by 1% of the time
where the time goes in v7:
time: 14.3 us; the launch traced here: 14.1 us
  starting transfers between devices  9.69 us (68%)
  Pallas kernels  3.27 us (23%)
  waiting for transfers between devices  1.13 us (8%)
    ppermute x3, starting transfers between devices, shards_by_trade(): far_in.append(lax.ppermute(piece, ('trade', 'path'), turns))  6.78 us
    ppermute x1, starting transfers between devices, shards_by_trade(): lax.ppermute(near, 'trade', [(at, at ^ NEAR) for at in range(owners)])  1.49 us
    pallas_call x1, Pallas kernels, shards_by_trade(): pl.pallas_call(price_late, out_shape=result, scratch_shapes=[pltpu.VMEM(t...  1.3 us
    ppermute x3, waiting for transfers between devices, shards_by_trade(): far_in.append(lax.ppermute(piece, ('trade', 'path'), turns))  1.1 us
    pallas_call x1, Pallas kernels, shards_by_trade(): pl.pallas_call(pack, out_shape=[message, near_message] + [message] * len(...  1.06 us
    ppermute x3, starting transfers between devices, shards_by_trade(): handed = [lax.ppermute(piece, 'path', swap) for piece in far_in]  0.97 us
    pallas_call x1, Pallas kernels, shards_by_trade(): pl.pallas_call(price_early, out_shape=[result, table, table], compiler_pa...  0.83 us
    ppermute x1, starting transfers between devices, shards_by_trade(): other_shocks = lax.ppermute(shocks, 'path', swap).reshape(2, dates_count)  0.45 us
  transfers between devices with their start and end apart: 8, of which 1 were waited for; matrix products, arithmetic and copies ran while one was open for 0% of the time, Pallas kernels for 13%

profile of v7, /device:TPU:0, one launch (start us, length us, event | category | flops | bytes accessed | tf_op | source)
XLA Modules:
  0.0 14.1 jit_solution(2983298406547333005)
XLA Ops:
  0.0 0.5 %collective-permute-start = (f32[2,2,1,1]{1,3,2,0:T(1,128)}, f32[2,2,1,1]{1,3,2,0:T(1,128)S(1)}, u32[]{:S(2)}, u32[]{:S(2)}) collective-permute-start(f32[2,2,1,1]{1,3,2,0:T(1,128)} %param.9), channel_id=1, source_target_pairs={{0,1},{1,0},{2,3},{3,2},{4,5},{5,4},{6,7},{7,6},{8,9},{9,8},{10,11... | collective-permute-start | bytes 56 | tf_op jit(solution)/shard_map/ppermute | solution.py:444
  0.5 1.1 %pack.1 = (f32[56,128]{1,0:T(8,128)S(1)}, f32[64,128]{1,0:T(8,128)S(1)}, f32[56,128]{1,0:T(8,128)S(1)}, f32[56,128]{1,0:T(8,128)S(1)}, f32[56,128]{1,0:T(8,128)S(1)}, /*index=5*/f32[3,8,128]{2,1,0:T(8,128)S(1)}) custom-call(s32[16,512]{1,0:T(8,128)} %bitcast.14, s32[16,512]{1,0:T(8,128)} %bitcast.15, s32[16,512]{1,0:T(8,128)} %bitcast.16, ...), custom_call_target="tpu_custom_call" | custom-call | tf_op jit(solution)/shard_map/pack/pallas_call | solution.py:459
  1.5 0.0 collective-permute-done
  1.5 0.1 add_shocks.1
  1.6 3.8 %collective-permute-start.1 = (f32[56,128]{1,0:T(8,128)S(1)}, f32[56,128]{1,0:T(8,128)S(1)}, u32[]{:S(2)}, u32[]{:S(2)}) collective-permute-start(f32[56,128]{1,0:T(8,128)S(1)} %get-tuple-element.21), channel_id=1, source_target_pairs={{0,6},{1,9},{2,4},{3,11},{4,2},{5,13},{6,0},{7,15},{8,14},{9,1},{1... | collective-permute-start | bytes 86024 | tf_op jit(solution)/shard_map/ppermute | solution.py:480
  5.4 0.4 %collective-permute-start.2 = (f32[56,128]{1,0:T(8,128)S(1)}, f32[56,128]{1,0:T(8,128)S(1)}, u32[]{:S(2)}, u32[]{:S(2)}) collective-permute-start(f32[56,128]{1,0:T(8,128)S(1)} %get-tuple-element.22), channel_id=1, source_target_pairs={{0,4},{1,13},{2,6},{3,15},{4,0},{5,9},{6,2},{7,11},{8,12},{9,5},{1... | collective-permute-start | bytes 86024 | tf_op jit(solution)/shard_map/ppermute | solution.py:480
  5.8 2.6 %collective-permute-start.3 = (f32[56,128]{1,0:T(8,128)S(1)}, f32[56,128]{1,0:T(8,128)S(1)}, u32[]{:S(2)}, u32[]{:S(2)}) collective-permute-start(f32[56,128]{1,0:T(8,128)S(1)} %get-tuple-element.23), channel_id=1, source_target_pairs={{0,10},{1,15},{2,8},{3,13},{4,14},{5,11},{6,12},{7,9},{8,2},{9,7},... | collective-permute-start | bytes 86024 | tf_op jit(solution)/shard_map/ppermute | solution.py:480
  8.4 1.5 %collective-permute-start.6 = (f32[64,128]{1,0:T(8,128)S(1)}, f32[64,128]{1,0:T(8,128)S(1)}, u32[]{:S(2)}, u32[]{:S(2)}) collective-permute-start(f32[64,128]{1,0:T(8,128)S(1)} %get-tuple-element.24), channel_id=1, source_target_pairs={{0,2},{2,0},{4,6},{6,4},{8,10},{10,8},{12,14},{14,12},{1,3},{3,1},... | collective-permute-start | bytes 98312 | tf_op jit(solution)/shard_map/ppermute | solution.py:469
  9.9 0.0 collective-permute-done.1.refs_1_
  9.9 0.0 collective-permute-start.4
  9.9 0.0 collective-permute-done.2.refs_2_
  9.9 0.5 %collective-permute-start.5 = (f32[56,128]{1,0:T(8,128)S(1)}, f32[56,128]{1,0:T(8,128)S(1)}, u32[]{:S(2)}, u32[]{:S(2)}) collective-permute-start(f32[56,128]{1,0:T(8,128)S(1)} %collective-permute-done.2.refs_2_), channel_id=1, source_target_pairs={{0,1},{1,0},{2,3},{3,2},{4,5},{5,4},{6,7},{7,6},{8,9},{9,8},{10,11... | collective-permute-start | bytes 86024 | tf_op jit(solution)/shard_map/ppermute | solution.py:481
  10.4 1.1 %collective-permute-done.3.refs_3_ = f32[56,128]{1,0:T(8,128)S(1)} collective-permute-done((f32[56,128]{1,0:T(8,128)S(1)}, f32[56,128]{1,0:T(8,128)S(1)}, u32[]{:S(2)}, u32[]{:S(2)}) %collective-permute-start.3) | collective-permute-done | bytes 28704 | tf_op jit(solution)/shard_map/ppermute | solution.py:480
  11.5 0.5 %collective-permute-start.7 = (f32[56,128]{1,0:T(8,128)S(1)}, f32[56,128]{1,0:T(8,128)S(1)}, u32[]{:S(2)}, u32[]{:S(2)}) collective-permute-start(f32[56,128]{1,0:T(8,128)S(1)} %collective-permute-done.3.refs_3_), channel_id=1, source_target_pairs={{0,1},{1,0},{2,3},{3,2},{4,5},{5,4},{6,7},{7,6},{8,9},{9,8},{10,11... | collective-permute-start | bytes 86024 | tf_op jit(solution)/shard_map/ppermute | solution.py:481
  12.0 0.0 collective-permute-done.4.refs_4_
  12.0 0.0 collective-permute-done.5.refs_5_
  12.0 0.8 %price_early.1 = (f32[16,32]{1,0:T(8,128)S(1)}, f32[16,128]{1,0:T(8,128)S(1)}, f32[16,128]{1,0:T(8,128)S(1)}) custom-call(f32[56,128]{1,0:T(8,128)S(1)} %get-tuple-element.17.refs_0_, f32[56,128]{1,0:T(8,128)S(1)} %collective-permute-done.1.refs_1_, f32[56,128]{1,0:T(8,128)S(1)} %collective-permute-done.2.refs_2_, ...), custom_call_target="tpu_custom_call" | custom-call | tf_op jit(solution)/shard_map/price_early/pallas_call | solution.py:485
  12.8 0.0 collective-permute-done.6.refs_6_
  12.8 0.0 collective-permute-done.7.refs_7_
  12.8 1.3 %price_late.1 = f32[16,32]{1,0:T(8,128)} custom-call(f32[56,128]{1,0:T(8,128)S(1)} %get-tuple-element.17.refs_0_, f32[56,128]{1,0:T(8,128)S(1)} %collective-permute-done.1.refs_1_, f32[56,128]{1,0:T(8,128)S(1)} %collective-permute-done.2.refs_2_, f32[56,128]{1,0:T(8,128)S(1)} %collective-permute-done.3.refs_3_, ...), custom_call_target="tpu_custom_call" | custom-call | tf_op jit(solution)/shard_map/price_late/pallas_call | solution.py:491
Async XLA Ops:
  0.0 1.5 %collective-permute-start = (f32[2,2,1,1]{1,3,2,0:T(1,128)}, f32[2,2,1,1]{1,3,2,0:T(1,128)S(1)}, u32[]{:S(2)}, u32[]{:S(2)}) collective-permute-start(f32[2,2,1,1]{1,3,2,0:T(1,128)} %param.9), channel_id=1, source_target_pairs={{0,1},{1,0},{2,3},{3,2},{4,5},{5,4},{6,7},{7,6},{8,9},{9,8},{10,11... | collective-permute-start | bytes 56 | tf_op jit(solution)/shard_map/ppermute | solution.py:444
  1.6 8.3 %collective-permute-start.1 = (f32[56,128]{1,0:T(8,128)S(1)}, f32[56,128]{1,0:T(8,128)S(1)}, u32[]{:S(2)}, u32[]{:S(2)}) collective-permute-start(f32[56,128]{1,0:T(8,128)S(1)} %get-tuple-element.21), channel_id=1, source_target_pairs={{0,6},{1,9},{2,4},{3,11},{4,2},{5,13},{6,0},{7,15},{8,14},{9,1},{1... | collective-permute-start | bytes 86024 | tf_op jit(solution)/shard_map/ppermute | solution.py:480
  5.4 4.5 %collective-permute-start.2 = (f32[56,128]{1,0:T(8,128)S(1)}, f32[56,128]{1,0:T(8,128)S(1)}, u32[]{:S(2)}, u32[]{:S(2)}) collective-permute-start(f32[56,128]{1,0:T(8,128)S(1)} %get-tuple-element.22), channel_id=1, source_target_pairs={{0,4},{1,13},{2,6},{3,15},{4,0},{5,9},{6,2},{7,11},{8,12},{9,5},{1... | collective-permute-start | bytes 86024 | tf_op jit(solution)/shard_map/ppermute | solution.py:480
  5.8 5.7 %collective-permute-start.3 = (f32[56,128]{1,0:T(8,128)S(1)}, f32[56,128]{1,0:T(8,128)S(1)}, u32[]{:S(2)}, u32[]{:S(2)}) collective-permute-start(f32[56,128]{1,0:T(8,128)S(1)} %get-tuple-element.23), channel_id=1, source_target_pairs={{0,10},{1,15},{2,8},{3,13},{4,14},{5,11},{6,12},{7,9},{8,2},{9,7},... | collective-permute-start | bytes 86024 | tf_op jit(solution)/shard_map/ppermute | solution.py:480
  8.4 4.4 %collective-permute-start.6 = (f32[64,128]{1,0:T(8,128)S(1)}, f32[64,128]{1,0:T(8,128)S(1)}, u32[]{:S(2)}, u32[]{:S(2)}) collective-permute-start(f32[64,128]{1,0:T(8,128)S(1)} %get-tuple-element.24), channel_id=1, source_target_pairs={{0,2},{2,0},{4,6},{6,4},{8,10},{10,8},{12,14},{14,12},{1,3},{3,1},... | collective-permute-start | bytes 98312 | tf_op jit(solution)/shard_map/ppermute | solution.py:469
  9.9 2.1 %collective-permute-start.4 = (f32[56,128]{1,0:T(8,128)S(1)}, f32[56,128]{1,0:T(8,128)S(1)}, u32[]{:S(2)}, u32[]{:S(2)}) collective-permute-start(f32[56,128]{1,0:T(8,128)S(1)} %collective-permute-done.1.refs_1_), channel_id=1, source_target_pairs={{0,1},{1,0},{2,3},{3,2},{4,5},{5,4},{6,7},{7,6},{8,9},{9,8},{10,11... | collective-permute-start | bytes 86024 | tf_op jit(solution)/shard_map/ppermute | solution.py:481
  9.9 2.1 %collective-permute-start.5 = (f32[56,128]{1,0:T(8,128)S(1)}, f32[56,128]{1,0:T(8,128)S(1)}, u32[]{:S(2)}, u32[]{:S(2)}) collective-permute-start(f32[56,128]{1,0:T(8,128)S(1)} %collective-permute-done.2.refs_2_), channel_id=1, source_target_pairs={{0,1},{1,0},{2,3},{3,2},{4,5},{5,4},{6,7},{7,6},{8,9},{9,8},{10,11... | collective-permute-start | bytes 86024 | tf_op jit(solution)/shard_map/ppermute | solution.py:481
  11.5 1.3 %collective-permute-start.7 = (f32[56,128]{1,0:T(8,128)S(1)}, f32[56,128]{1,0:T(8,128)S(1)}, u32[]{:S(2)}, u32[]{:S(2)}) collective-permute-start(f32[56,128]{1,0:T(8,128)S(1)} %collective-permute-done.3.refs_3_), channel_id=1, source_target_pairs={{0,1},{1,0},{2,3},{3,2},{4,5},{5,4},{6,7},{7,6},{8,9},{9,8},{10,11... | collective-permute-start | bytes 86024 | tf_op jit(solution)/shard_map/ppermute | solution.py:481

commit v8 on v6

--- a/solution.py
+++ b/solution.py
@@ -400,15 +400,19 @@
 def net(refs, totals):
     extra = FIELDS * SLOTS_TILE
     set_index = iota((SET_DEV, LANES), 0).astype(jnp.float32)
-    one_hot = jnp.concatenate(
-        [(set_index == ref[extra : extra + 1, :]).astype(jnp.bfloat16) for ref in refs], axis=1
-    )
-    netted = lax.dot_general(
-        split(jnp.concatenate(totals, axis=1), 3),
-        one_hot,
-        (((1,), (1,)), ((), ())),
-        preferred_element_type=jnp.float32,
-    )
+    netted = None
+    for group in range(0, len(refs), 4):
+        cut = slice(group, group + 4)
+        one_hot = jnp.concatenate(
+            [(set_index == ref[extra : extra + 1, :]).astype(jnp.bfloat16) for ref in refs[cut]], axis=1
+        )
+        product = lax.dot_general(
+            split(jnp.concatenate(totals[cut], axis=1), 3),
+            one_hot,
+            (((1,), (1,)), ((), ())),
+            preferred_element_type=jnp.float32,
+        )
+        netted = product if netted is None else netted + product
     return add_parts(netted, 3)
 
 

time: 14.3 us -> 14.3 us (level)
  no operation moved by 1% of the time
where the time goes in v8:
time: 14.3 us; the launch traced here: 14.1 us
  starting transfers between devices  9.69 us (68%)
  Pallas kernels  3.28 us (23%)
  waiting for transfers between devices  1.14 us (8%)
    ppermute x3, starting transfers between devices, shards_by_trade(): far_in.append(lax.ppermute(piece, ('trade', 'path'), turns))  6.78 us
    ppermute x1, starting transfers between devices, shards_by_trade(): lax.ppermute(near, 'trade', [(at, at ^ NEAR) for at in range(owners)])  1.49 us
    pallas_call x1, Pallas kernels, shards_by_trade(): pl.pallas_call(price_late, out_shape=result, scratch_shapes=[pltpu.VMEM(t...  1.33 us
    ppermute x3, waiting for transfers between devices, shards_by_trade(): far_in.append(lax.ppermute(piece, ('trade', 'path'), turns))  1.1 us
    pallas_call x1, Pallas kernels, shards_by_trade(): pl.pallas_call(pack, out_shape=[message, near_message] + [message] * len(...  1.06 us
    ppermute x3, starting transfers between devices, shards_by_trade(): handed = [lax.ppermute(piece, 'path', swap) for piece in far_in]  0.97 us
    pallas_call x1, Pallas kernels, shards_by_trade(): pl.pallas_call(price_early, out_shape=[result, table, table], compiler_pa...  0.81 us
    ppermute x1, starting transfers between devices, shards_by_trade(): other_shocks = lax.ppermute(shocks, 'path', swap).reshape(2, dates_count)  0.45 us
  transfers between devices with their start and end apart: 8, of which 1 were waited for; matrix products, arithmetic and copies ran while one was open for 0% of the time, Pallas kernels for 13%

profile of v8, /device:TPU:0, one launch (start us, length us, event | category | flops | bytes accessed | tf_op | source)
XLA Modules:
  0.0 14.1 jit_solution(5937567112023401908)
XLA Ops:
  0.0 0.5 %collective-permute-start = (f32[2,2,1,1]{1,3,2,0:T(1,128)}, f32[2,2,1,1]{1,3,2,0:T(1,128)S(1)}, u32[]{:S(2)}, u32[]{:S(2)}) collective-permute-start(f32[2,2,1,1]{1,3,2,0:T(1,128)} %param.9), channel_id=1, source_target_pairs={{0,1},{1,0},{2,3},{3,2},{4,5},{5,4},{6,7},{7,6},{8,9},{9,8},{10,11... | collective-permute-start | bytes 56 | tf_op jit(solution)/shard_map/ppermute | solution.py:448
  0.5 1.1 %pack.1 = (f32[56,128]{1,0:T(8,128)S(1)}, f32[64,128]{1,0:T(8,128)S(1)}, f32[56,128]{1,0:T(8,128)S(1)}, f32[56,128]{1,0:T(8,128)S(1)}, f32[56,128]{1,0:T(8,128)S(1)}, /*index=5*/f32[3,8,128]{2,1,0:T(8,128)S(1)}) custom-call(s32[16,512]{1,0:T(8,128)} %bitcast.14, s32[16,512]{1,0:T(8,128)} %bitcast.15, s32[16,512]{1,0:T(8,128)} %bitcast.16, ...), custom_call_target="tpu_custom_call" | custom-call | tf_op jit(solution)/shard_map/pack/pallas_call | solution.py:463
  1.5 0.0 collective-permute-done
  1.5 0.1 add_shocks.1
  1.6 2.8 %collective-permute-start.1 = (f32[56,128]{1,0:T(8,128)S(1)}, f32[56,128]{1,0:T(8,128)S(1)}, u32[]{:S(2)}, u32[]{:S(2)}) collective-permute-start(f32[56,128]{1,0:T(8,128)S(1)} %get-tuple-element.21), channel_id=1, source_target_pairs={{0,4},{1,9},{2,6},{3,11},{4,0},{5,13},{6,2},{7,15},{8,12},{9,1},{1... | collective-permute-start | bytes 86024 | tf_op jit(solution)/shard_map/ppermute | solution.py:484
  4.5 1.4 %collective-permute-start.2 = (f32[56,128]{1,0:T(8,128)S(1)}, f32[56,128]{1,0:T(8,128)S(1)}, u32[]{:S(2)}, u32[]{:S(2)}) collective-permute-start(f32[56,128]{1,0:T(8,128)S(1)} %get-tuple-element.22), channel_id=1, source_target_pairs={{0,6},{1,13},{2,4},{3,15},{4,2},{5,9},{6,0},{7,11},{8,14},{9,5},{1... | collective-permute-start | bytes 86024 | tf_op jit(solution)/shard_map/ppermute | solution.py:484
  5.8 2.6 %collective-permute-start.3 = (f32[56,128]{1,0:T(8,128)S(1)}, f32[56,128]{1,0:T(8,128)S(1)}, u32[]{:S(2)}, u32[]{:S(2)}) collective-permute-start(f32[56,128]{1,0:T(8,128)S(1)} %get-tuple-element.23), channel_id=1, source_target_pairs={{0,10},{1,15},{2,8},{3,13},{4,14},{5,11},{6,12},{7,9},{8,2},{9,7},... | collective-permute-start | bytes 86024 | tf_op jit(solution)/shard_map/ppermute | solution.py:484
  8.4 1.5 %collective-permute-start.6 = (f32[64,128]{1,0:T(8,128)S(1)}, f32[64,128]{1,0:T(8,128)S(1)}, u32[]{:S(2)}, u32[]{:S(2)}) collective-permute-start(f32[64,128]{1,0:T(8,128)S(1)} %get-tuple-element.24), channel_id=1, source_target_pairs={{0,2},{2,0},{4,6},{6,4},{8,10},{10,8},{12,14},{14,12},{1,3},{3,1},... | collective-permute-start | bytes 98312 | tf_op jit(solution)/shard_map/ppermute | solution.py:473
  9.9 0.0 collective-permute-done.1.refs_1_
  9.9 0.0 collective-permute-start.4
  9.9 0.0 collective-permute-done.2.refs_2_
  9.9 0.5 %collective-permute-start.5 = (f32[56,128]{1,0:T(8,128)S(1)}, f32[56,128]{1,0:T(8,128)S(1)}, u32[]{:S(2)}, u32[]{:S(2)}) collective-permute-start(f32[56,128]{1,0:T(8,128)S(1)} %collective-permute-done.2.refs_2_), channel_id=1, source_target_pairs={{0,1},{1,0},{2,3},{3,2},{4,5},{5,4},{6,7},{7,6},{8,9},{9,8},{10,11... | collective-permute-start | bytes 86024 | tf_op jit(solution)/shard_map/ppermute | solution.py:485
  10.4 1.1 %collective-permute-done.3.refs_3_ = f32[56,128]{1,0:T(8,128)S(1)} collective-permute-done((f32[56,128]{1,0:T(8,128)S(1)}, f32[56,128]{1,0:T(8,128)S(1)}, u32[]{:S(2)}, u32[]{:S(2)}) %collective-permute-start.3) | collective-permute-done | bytes 28704 | tf_op jit(solution)/shard_map/ppermute | solution.py:484
  11.5 0.5 %collective-permute-start.7 = (f32[56,128]{1,0:T(8,128)S(1)}, f32[56,128]{1,0:T(8,128)S(1)}, u32[]{:S(2)}, u32[]{:S(2)}) collective-permute-start(f32[56,128]{1,0:T(8,128)S(1)} %collective-permute-done.3.refs_3_), channel_id=1, source_target_pairs={{0,1},{1,0},{2,3},{3,2},{4,5},{5,4},{6,7},{7,6},{8,9},{9,8},{10,11... | collective-permute-start | bytes 86024 | tf_op jit(solution)/shard_map/ppermute | solution.py:485
  12.0 0.0 collective-permute-done.4.refs_4_
  12.0 0.0 collective-permute-done.5.refs_5_
  12.0 0.8 %price_early.1 = (f32[16,32]{1,0:T(8,128)S(1)}, f32[16,128]{1,0:T(8,128)S(1)}, f32[16,128]{1,0:T(8,128)S(1)}) custom-call(f32[56,128]{1,0:T(8,128)S(1)} %get-tuple-element.17.refs_0_, f32[56,128]{1,0:T(8,128)S(1)} %collective-permute-done.1.refs_1_, f32[56,128]{1,0:T(8,128)S(1)} %collective-permute-done.2.refs_2_, ...), custom_call_target="tpu_custom_call" | custom-call | tf_op jit(solution)/shard_map/price_early/pallas_call | solution.py:489
  12.8 0.0 collective-permute-done.6.refs_6_
  12.8 0.0 collective-permute-done.7.refs_7_
  12.8 1.3 %price_late.1 = f32[16,32]{1,0:T(8,128)} custom-call(f32[56,128]{1,0:T(8,128)S(1)} %get-tuple-element.17.refs_0_, f32[56,128]{1,0:T(8,128)S(1)} %collective-permute-done.1.refs_1_, f32[56,128]{1,0:T(8,128)S(1)} %collective-permute-done.2.refs_2_, f32[56,128]{1,0:T(8,128)S(1)} %collective-permute-done.3.refs_3_, ...), custom_call_target="tpu_custom_call" | custom-call | tf_op jit(solution)/shard_map/price_late/pallas_call | solution.py:495
Async XLA Ops:
  0.0 1.5 %collective-permute-start = (f32[2,2,1,1]{1,3,2,0:T(1,128)}, f32[2,2,1,1]{1,3,2,0:T(1,128)S(1)}, u32[]{:S(2)}, u32[]{:S(2)}) collective-permute-start(f32[2,2,1,1]{1,3,2,0:T(1,128)} %param.9), channel_id=1, source_target_pairs={{0,1},{1,0},{2,3},{3,2},{4,5},{5,4},{6,7},{7,6},{8,9},{9,8},{10,11... | collective-permute-start | bytes 56 | tf_op jit(solution)/shard_map/ppermute | solution.py:448
  1.6 8.3 %collective-permute-start.1 = (f32[56,128]{1,0:T(8,128)S(1)}, f32[56,128]{1,0:T(8,128)S(1)}, u32[]{:S(2)}, u32[]{:S(2)}) collective-permute-start(f32[56,128]{1,0:T(8,128)S(1)} %get-tuple-element.21), channel_id=1, source_target_pairs={{0,4},{1,9},{2,6},{3,11},{4,0},{5,13},{6,2},{7,15},{8,12},{9,1},{1... | collective-permute-start | bytes 86024 | tf_op jit(solution)/shard_map/ppermute | solution.py:484
  4.5 5.4 %collective-permute-start.2 = (f32[56,128]{1,0:T(8,128)S(1)}, f32[56,128]{1,0:T(8,128)S(1)}, u32[]{:S(2)}, u32[]{:S(2)}) collective-permute-start(f32[56,128]{1,0:T(8,128)S(1)} %get-tuple-element.22), channel_id=1, source_target_pairs={{0,6},{1,13},{2,4},{3,15},{4,2},{5,9},{6,0},{7,11},{8,14},{9,5},{1... | collective-permute-start | bytes 86024 | tf_op jit(solution)/shard_map/ppermute | solution.py:484
  5.8 5.7 %collective-permute-start.3 = (f32[56,128]{1,0:T(8,128)S(1)}, f32[56,128]{1,0:T(8,128)S(1)}, u32[]{:S(2)}, u32[]{:S(2)}) collective-permute-start(f32[56,128]{1,0:T(8,128)S(1)} %get-tuple-element.23), channel_id=1, source_target_pairs={{0,10},{1,15},{2,8},{3,13},{4,14},{5,11},{6,12},{7,9},{8,2},{9,7},... | collective-permute-start | bytes 86024 | tf_op jit(solution)/shard_map/ppermute | solution.py:484
  8.4 4.4 %collective-permute-start.6 = (f32[64,128]{1,0:T(8,128)S(1)}, f32[64,128]{1,0:T(8,128)S(1)}, u32[]{:S(2)}, u32[]{:S(2)}) collective-permute-start(f32[64,128]{1,0:T(8,128)S(1)} %get-tuple-element.24), channel_id=1, source_target_pairs={{0,2},{2,0},{4,6},{6,4},{8,10},{10,8},{12,14},{14,12},{1,3},{3,1},... | collective-permute-start | bytes 98312 | tf_op jit(solution)/shard_map/ppermute | solution.py:473
  9.9 2.1 %collective-permute-start.4 = (f32[56,128]{1,0:T(8,128)S(1)}, f32[56,128]{1,0:T(8,128)S(1)}, u32[]{:S(2)}, u32[]{:S(2)}) collective-permute-start(f32[56,128]{1,0:T(8,128)S(1)} %collective-permute-done.1.refs_1_), channel_id=1, source_target_pairs={{0,1},{1,0},{2,3},{3,2},{4,5},{5,4},{6,7},{7,6},{8,9},{9,8},{10,11... | collective-permute-start | bytes 86024 | tf_op jit(solution)/shard_map/ppermute | solution.py:485
  9.9 2.1 %collective-permute-start.5 = (f32[56,128]{1,0:T(8,128)S(1)}, f32[56,128]{1,0:T(8,128)S(1)}, u32[]{:S(2)}, u32[]{:S(2)}) collective-permute-start(f32[56,128]{1,0:T(8,128)S(1)} %collective-permute-done.2.refs_2_), channel_id=1, source_target_pairs={{0,1},{1,0},{2,3},{3,2},{4,5},{5,4},{6,7},{7,6},{8,9},{9,8},{10,11... | collective-permute-start | bytes 86024 | tf_op jit(solution)/shard_map/ppermute | solution.py:485
  11.5 1.3 %collective-permute-start.7 = (f32[56,128]{1,0:T(8,128)S(1)}, f32[56,128]{1,0:T(8,128)S(1)}, u32[]{:S(2)}, u32[]{:S(2)}) collective-permute-start(f32[56,128]{1,0:T(8,128)S(1)} %collective-permute-done.3.refs_3_), channel_id=1, source_target_pairs={{0,1},{1,0},{2,3},{3,2},{4,5},{5,4},{6,7},{7,6},{8,9},{9,8},{10,11... | collective-permute-start | bytes 86024 | tf_op jit(solution)/shard_map/ppermute | solution.py:485
